TPU v7x, 512 devices: a whole 4x8x8 slice. The times are simulated.
512 devices in a mesh: box: 64 (over y, x, core), dir: 8 (over z).
Axes of the slice: x: 4, y: 8, z: 8, core: 2. Of those that a mesh axis runs over, the one named last changes fastest.
Arguments:
- currents: bfloat16 [2, 128, 16384], P(None, None, 'box'), may hold values from -6 to 6
- box_code: int32 [16384], P('box'), may hold values from 0 to 255, as said below
- box_count: int32 [64], P('box'), may hold values from 76 to 256, as said below
- radiation: bfloat16 [2, 128, 128], replicated, may hold values from -0.375 to 0.375
- near_block: bfloat16 [9, 2, 128, 128], replicated, may hold values from -0.125 to 0.125
- translation: float32 [40, 2, 16, 32], P(None, None, None, 'dir'), may hold values from -1.2 to 1.2
Outputs:
- result: bfloat16 [2, 128, 16384], P(None, None, ('box', 'dir'))
Inputs may be any that keep to these rules, and one draw needn't show every extreme that they name: `box_code`: for each block the 256 entries are the Morton codes of its 16 x 16 cells, each once; the first box_count entries, ascending, are the live boxes. `box_count`: some block is full and some block holds exactly the least count.
All inputs are finite; a program needn't handle non-finite values.
Results may differ from a plain program's by a relative error of at most 0.0016.
Values may be sent and summed in bfloat16 or wider, within the bound.
A program may use at most 64 MiB of HBM per device.

v0:
```python
import math

import jax
import jax.numpy as jnp
from jax import lax
from jax.sharding import PartitionSpec as P

NT0 = 8
NP0 = 16
NT1 = 16
NP1 = 32
BSIDE = 16
RIM = 6
BOX_DEV = 256


highest = lax.Precision.HIGHEST
wave_size = math.pi


def shifted(x, axis, by):
    size = lax.axis_size(axis)
    pairs = [(i, i + by) for i in range(size) if 0 <= i + by < size]
    return lax.ppermute(x, axis, pairs)


def padded(block, sides, width):
    for axis, dim in sides:
        count = lax.axis_size(axis)
        forward = [(i, i + 1) for i in range(count - 1)]
        forward.append((count - 1, 0))
        backward = [(target, source) for source, target in forward]
        low = lax.ppermute(
            lax.slice_in_dim(block, block.shape[dim] - width, None, axis=dim), axis, forward
        )
        high = lax.ppermute(lax.slice_in_dim(block, 0, width, axis=dim), axis, backward)
        block = jnp.concatenate([low, block, high], axis=dim)
    return block


def morton_split(code):
    row_index = jnp.zeros_like(code)
    column_index = jnp.zeros_like(code)
    for bit_place in range(6):
        column_index = column_index + ((code >> 2 * bit_place & 1) << bit_place)
        row_index = row_index + ((code >> 2 * bit_place + 1 & 1) << bit_place)
    return (row_index, column_index)


def lagrange(offset, node):
    first = -(offset - 1.0) * (offset - 2.0) * (offset - 3.0) / 6.0
    second = offset * (offset - 2.0) * (offset - 3.0) / 2.0
    third = -offset * (offset - 1.0) * (offset - 3.0) / 2.0
    fourth = offset * (offset - 1.0) * (offset - 2.0) / 6.0
    return (
        jnp.where(node == 0, first, 0.0)
        + jnp.where(node == 1, second, 0.0)
        + jnp.where(node == 2, third, 0.0)
        + jnp.where(node == 3, fourth, 0.0)
    )


def theta_table(coarse_count, fine_count):
    coarse = jnp.arange(coarse_count, dtype=jnp.int32)[:, None]
    fine = jnp.arange(fine_count, dtype=jnp.int32)[None, :]
    twice = 2 * coarse - 1
    base = jnp.clip(twice // 4 - 1, 0, fine_count - 4)
    offset = (twice - 4 * base).astype(jnp.float32) / 4.0
    return lagrange(offset, fine - base)


def phi_table(coarse, fine):
    twice = 2 * coarse[:, None] - 1
    base = twice // 4 - 1
    offset = (twice - 4 * base).astype(jnp.float32) / 4.0
    node = fine[None, :] - base
    return lagrange(offset, node)


def phase_angle(theta_index, phi_index, theta_count, phi_count):
    theta = (theta_index.astype(jnp.float32) + 0.5) * math.pi / theta_count
    azimuth = (phi_index.astype(jnp.float32) + 0.5) * 2.0 * math.pi / phi_count
    along_column = jnp.sin(theta)[:, None] * jnp.cos(azimuth)[None, :]
    along_row = jnp.sin(theta)[:, None] * jnp.sin(azimuth)[None, :]
    halves = jnp.array([-0.5, 0.5], dtype=jnp.float32)
    return wave_size * (
        along_row[:, :, None, None] * halves[:, None]
        + along_column[:, :, None, None] * halves[None, :]
    )


def displacements():
    return [
        (offset_row, offset_column)
        for offset_row in range(-3, 4)
        for offset_column in range(-3, 4)
        if max(abs(offset_row), abs(offset_column)) >= 2
    ]


def gather_children(upper, angle, cells_side):
    parents_side = cells_side // 2
    shaped = upper.reshape(2, upper.shape[1], upper.shape[2], parents_side, 2, parents_side, 2)
    cosine = jnp.cos(angle)[:, :, None, :, None, :]
    sine = jnp.sin(angle)[:, :, None, :, None, :]
    real_part = jnp.sum(shaped[0] * cosine + shaped[1] * sine, axis=(3, 5))
    imaginary = jnp.sum(shaped[1] * cosine - shaped[0] * sine, axis=(3, 5))
    return jnp.stack([real_part, imaginary])


def spread_children(incoming, angle):
    cosine = jnp.cos(angle)[:, :, None, :, None, :]
    sine = jnp.sin(angle)[:, :, None, :, None, :]
    source_real = incoming[0][:, :, :, None, :, None]
    source_imag = incoming[1][:, :, :, None, :, None]
    real_part = source_real * cosine - source_imag * sine
    imaginary = source_imag * cosine + source_real * sine
    stacked = jnp.stack([real_part, imaginary])
    return stacked.reshape(2, stacked.shape[1], stacked.shape[2], -1)


def translate(parent, translation, global_rows, global_columns, count):
    total = jnp.zeros(parent.shape[:3] + (count, count), jnp.float32)
    for number, (offset_row, offset_column) in enumerate(displacements()):
        source = parent[
            :,
            :,
            :,
            3 + offset_row : 3 + offset_row + count,
            3 + offset_column : 3 + offset_column + count,
        ]
        keep_row = jnp.abs((global_rows + offset_row) // 2 - global_rows // 2) <= 1
        keep_column = jnp.abs((global_columns + offset_column) // 2 - global_columns // 2) <= 1
        keep = keep_row[:, None] & keep_column[None, :]
        op_real = translation[number, 0][:, :, None, None]
        op_imag = translation[number, 1][:, :, None, None]
        real_part = op_real * source[0] - op_imag * source[1]
        imaginary = op_real * source[1] + op_imag * source[0]
        total = total + jnp.where(keep, jnp.stack([real_part, imaginary]), 0.0)
    return total


def receive(radiation_wide, lower_flat):
    far_real = jnp.einsum(
        "ku,kn->un", radiation_wide[0], lower_flat[0], precision=highest
    ) + jnp.einsum("ku,kn->un", radiation_wide[1], lower_flat[1], precision=highest)
    far_imag = jnp.einsum(
        "ku,kn->un", radiation_wide[0], lower_flat[1], precision=highest
    ) - jnp.einsum("ku,kn->un", radiation_wide[1], lower_flat[0], precision=highest)
    return jnp.stack([far_real, far_imag])


def complex_stack(rad_part):
    return jnp.concatenate(
        [
            jnp.concatenate([rad_part[0], -rad_part[1]], axis=1),
            jnp.concatenate([rad_part[1], rad_part[0]], axis=1),
        ],
        axis=0,
    )


def edge_piece(array, step_row, step_column, width):
    rows_total = array.shape[-2]
    columns_total = array.shape[-1]
    if step_row < 0:
        array = array[..., rows_total - width :, :]
    elif step_row > 0:
        array = array[..., :width, :]
    if step_column < 0:
        array = array[..., columns_total - width :]
    elif step_column > 0:
        array = array[..., :width]
    return array


def on_device(currents, box_code, box_count, radiation, near_block, translation):
    blocks_across = math.isqrt(lax.axis_size("box"))
    dir_count = lax.axis_size("dir")
    block_index = lax.axis_index("box")
    group_index = lax.axis_index("dir")
    block_row = block_index // blocks_across
    block_column = block_index % blocks_across
    unit_count = currents.shape[1]
    extent = BSIDE + 2 * RIM
    parents_side = BSIDE // 2
    local_phi = NP0 // dir_count
    coarse_local = NP1 // dir_count
    own_slots = BOX_DEV // dir_count
    slot_ids = jnp.arange(BOX_DEV, dtype=jnp.int32)
    live = slot_ids < box_count[0]
    row_index, column_index = morton_split(box_code)
    cell = row_index * BSIDE + column_index
    masked = jnp.where(live[None, None, :], currents, jnp.zeros_like(currents))
    field = jnp.zeros_like(currents).at[:, :, cell].set(masked).reshape(2, unit_count, BSIDE, BSIDE)
    band_list = []
    for step_row in (-1, 0, 1):
        pieces = []
        for step_column in (-1, 0, 1):
            if step_row == 0 and step_column == 0:
                pieces.append(field)
            else:
                outgoing = edge_piece(field, step_row, step_column, RIM)
                arrived = shifted(outgoing, "box", -(step_row * blocks_across + step_column))
                pieces.append(
                    jnp.where(
                        (block_row + step_row >= 0)
                        & (block_row + step_row < blocks_across)
                        & (block_column + step_column >= 0)
                        & (block_column + step_column < blocks_across),
                        arrived,
                        jnp.zeros_like(arrived),
                    )
                )
        band_list.append(jnp.concatenate(pieces, axis=3))
    extended = jnp.concatenate(band_list, axis=2)
    rad_grid = radiation.reshape(2, NT0, NP0, unit_count)
    rad_local = lax.dynamic_slice_in_dim(rad_grid, group_index * local_phi, local_phi, 2).reshape(
        2, NT0 * local_phi, unit_count
    )
    flat_field = extended.reshape(2 * unit_count, extent * extent)
    fine_wide = group_index * local_phi - 2 + jnp.arange(local_phi + 4, dtype=jnp.int32)
    pattern = jnp.dot(
        complex_stack(rad_local), flat_field, preferred_element_type=jnp.float32
    ).reshape(2, NT0, local_phi, extent * extent)
    padded_pattern = padded(pattern, (("dir", 2),), 2)
    theta_weight = theta_table(NT1, NT0)
    coarse_ids = group_index * coarse_local + jnp.arange(coarse_local, dtype=jnp.int32)
    up_weight = phi_table(coarse_ids, fine_wide)
    upper = jnp.einsum("it,ctpn->cipn", theta_weight, padded_pattern, precision=highest)
    upper = jnp.einsum("qp,cipn->ciqn", up_weight, upper, precision=highest)
    angle = phase_angle(jnp.arange(NT1, dtype=jnp.int32), coarse_ids, NT1, NP1)
    parent = gather_children(upper, angle, extent)
    local_rows = jnp.arange(parents_side, dtype=jnp.int32)
    incoming = translate(
        parent,
        translation,
        block_row * parents_side + local_rows,
        block_column * parents_side + local_rows,
        parents_side,
    )
    flat_incoming = incoming.reshape(2, NT1, coarse_local, parents_side * parents_side)
    wide_incoming = padded(flat_incoming, (("dir", 2),), 3)
    coarse_wide = group_index * coarse_local - 3 + jnp.arange(coarse_local + 6, dtype=jnp.int32)
    wide_angle = phase_angle(jnp.arange(NT1, dtype=jnp.int32), coarse_wide, NT1, NP1)
    child = spread_children(
        wide_incoming.reshape(2, NT1, coarse_local + 6, parents_side, parents_side), wide_angle
    )
    fine_own = group_index * local_phi + jnp.arange(local_phi, dtype=jnp.int32)
    back_weight = phi_table(coarse_wide, fine_own)
    lower = 0.25 * jnp.einsum("it,ciqn->ctqn", theta_weight, child, precision=highest)
    lower = jnp.einsum("qp,ctqn->ctpn", back_weight, lower, precision=highest)
    by_slot = jnp.take(lower, cell, axis=3)
    by_slot = jnp.where(live[None, None, None, :], by_slot, 0.0)
    partial_far = receive(
        rad_local.astype(jnp.float32), by_slot.reshape(2, NT0 * local_phi, BOX_DEV)
    )
    far = lax.psum_scatter(partial_far, "dir", scatter_dimension=2, tiled=True)
    first_slot = group_index * own_slots
    own_rows = lax.dynamic_slice_in_dim(row_index, first_slot, own_slots)
    own_columns = lax.dynamic_slice_in_dim(column_index, first_slot, own_slots)
    own_live = lax.dynamic_slice_in_dim(live, first_slot, own_slots)
    positions = jnp.stack(
        [
            (own_rows + RIM + step_row) * extent + own_columns + RIM + step_column
            for step_row in (-1, 0, 1)
            for step_column in (-1, 0, 1)
        ]
    )
    gathered = jnp.take(
        extended.reshape(2, unit_count, extent * extent), positions.reshape(-1), axis=2
    )
    gathered = gathered.reshape(2, unit_count, 9, own_slots)
    near_real = jnp.einsum(
        "duv,vds->us", near_block[:, 0], gathered[0], preferred_element_type=jnp.float32
    ) - jnp.einsum("duv,vds->us", near_block[:, 1], gathered[1], preferred_element_type=jnp.float32)
    near_imag = jnp.einsum(
        "duv,vds->us", near_block[:, 0], gathered[1], preferred_element_type=jnp.float32
    ) + jnp.einsum("duv,vds->us", near_block[:, 1], gathered[0], preferred_element_type=jnp.float32)
    total = jnp.stack([near_real, near_imag]) + far
    return jnp.where(own_live[None, None, :], total, 0.0).astype(jnp.bfloat16)


def solution(mesh):
    placed = (P(None, None, "box"), P("box"), P("box"), P(), P(), P(None, None, None, "dir"))
    return jax.shard_map(
        on_device,
        mesh=mesh,
        in_specs=placed,
        out_specs=P(None, None, ("box", "dir")),
        check_vma=False,
    )
```

profile of v0, /device:TPU:4, one launch (start us, length us, event | category | flops | bytes accessed | tf_op | source)
XLA Modules:
  0.0 199.0 jit_solution(15298595175968955571)
XLA Ops:
  6.5 1.3 compare_and_fusion
  8.5 1.0 copy.374
  10.0 7.2 %scatter_fusion = bf16[2,128,256]{1,0,2:T(2,128)(2,1)S(1)} fusion(bf16[2,128,256]{1,0,2:T(2,128)(2,1)S(1)} %broadcast.2745, s32[256]{0:T(256)S(1)} %get-tuple-element.14, bf16[256,2,128]{2,1,0:T(2,128)(2,1)S(1)} %fusion.30), kind=kCustom, calls=%fused_computation.2 | custom fusion | bytes 394240 | tf_op jit(solution)/shard_map/scatter | solution.py:195
  17.2 1.3 collective-permute-start.5
  18.5 5.2 %collective-permute-start.2 = (bf16[2,128,6,6]{1,0,3,2:T(2,128)(2,1)S(1)}, bf16[2,128,6,6]{1,0,3,2:T(2,128)(2,1)S(1)}, u32[]{:S(2)}, u32[]{:S(2)}) collective-permute-start(bf16[2,128,6,6]{1,0,3,2:T(2,128)(2,1)S(1)} %get-tuple-element.160), channel_id=1, source_target_pairs={{0,56},{8,64},{16,72},{24,80},{32,88},{40,96},{48,104},{56,112},{6... | collective-permute-start | bytes 55304 | tf_op jit(solution)/shard_map/ppermute | solution.py:24
  23.7 2.1 %collective-permute-start = (bf16[2,128,6,6]{1,0,3,2:T(2,128)(2,1)S(1)}, bf16[2,128,6,6]{1,0,3,2:T(2,128)(2,1)S(1)}, u32[]{:S(2)}, u32[]{:S(2)}) collective-permute-start(bf16[2,128,6,6]{1,0,3,2:T(2,128)(2,1)S(1)} %get-tuple-element.157), channel_id=1, source_target_pairs={{0,72},{8,80},{16,88},{24,96},{32,104},{40,112},{48,120},{56,128},... | collective-permute-start | bytes 55304 | tf_op jit(solution)/shard_map/ppermute | solution.py:24
  25.9 1.3 collective-permute-start.7
  27.2 4.4 %collective-permute-start.4 = (bf16[2,128,16,6]{1,0,3,2:T(2,128)(2,1)S(1)}, bf16[2,128,16,6]{1,0,3,2:T(2,128)(2,1)S(1)}, u32[]{:S(2)}, u32[]{:S(2)}) collective-permute-start(bf16[2,128,16,6]{1,0,3,2:T(2,128)(2,1)S(1)} %get-tuple-element.164), channel_id=1, source_target_pairs={{8,0},{16,8},{24,16},{32,24},{40,32},{48,40},{56,48},{64,56},{72,6... | collective-permute-start | bytes 147464 | tf_op jit(solution)/shard_map/ppermute | solution.py:24
  36.5 0.7 constant_dynamic-slice_fusion.1
  39.9 0.9 fusion.73
  61.3 1.9 collective-permute-start.3
  63.3 4.5 %collective-permute-start.1 = (bf16[2,128,6,16]{1,0,3,2:T(2,128)(2,1)S(1)}, bf16[2,128,6,16]{1,0,3,2:T(2,128)(2,1)S(1)}, u32[]{:S(2)}, u32[]{:S(2)}) collective-permute-start(bf16[2,128,6,16]{1,0,3,2:T(2,128)(2,1)S(1)} %get-tuple-element.161), channel_id=1, source_target_pairs={{0,64},{8,72},{16,80},{24,88},{32,96},{40,104},{48,112},{56,120},{... | collective-permute-start | bytes 147464 | tf_op jit(solution)/shard_map/ppermute | solution.py:24
  67.8 1.3 collective-permute-start.6
  69.9 4.5 %collective-permute-done.6 = bf16[2,128,6,16]{1,0,3,2:T(2,128)(2,1)S(1)} collective-permute-done((bf16[2,128,6,16]{1,0,3,2:T(2,128)(2,1)S(1)}, bf16[2,128,6,16]{1,0,3,2:T(2,128)(2,1)S(1)}, u32[]{:S(2)}, u32[]{:S(2)}) %collective-permute-start.6) | collective-permute-done | bytes 49184 | tf_op jit(solution)/shard_map/ppermute | solution.py:24
  74.4 5.7 %maximum_maximum_fusion = bf16[2,128,28,28]{1,0,3,2:T(2,128)(2,1)S(1)} fusion(bf16[2,128,6,6]{1,0,3,2:T(2,128)(2,1)S(1)} %broadcast_select_fusion.6, bf16[2,128,6,16]{1,0,3,2:T(2,128)(2,1)S(1)} %broadcast_select_fusion.2, bf16[2,128,6,6]{1,0,3,2:T(2,128)(2,1)S(1)} %broadcast_select_fusion.7, bf16[2,128,16,6]{1,0,3,2:T(2,128)(2,1)S(1)} %broadcast_select_fusion.3, ...), kind=kLoop, calls=%fused_computation.29 | loop fusion | flops 1605632 | bytes 802816 | tf_op jit(solution)/shard_map/concatenate | solution.py:216
  80.6 4.3 %collective-permute-start.8 = (f32[2,8,2,784]{3,1,2,0:T(8,128)S(1)}, f32[2,8,2,784]{3,1,2,0:T(8,128)S(1)}, u32[]{:S(2)}, u32[]{:S(2)}) collective-permute-start(f32[2,8,2,784]{3,1,2,0:T(8,128)S(1)} %fusion.10), channel_id=1, source_target_pairs={{0,1},{1,2},{2,3},{3,4},{4,5},{5,6},{6,7},{7,0},{8,9},{9,10},{10,1... | collective-permute-start | bytes 301064 | tf_op jit(solution)/shard_map/ppermute | solution.py:33
  84.9 8.8 %collective-permute-start.9 = (f32[2,8,2,784]{3,1,2,0:T(8,128)S(1)}, f32[2,8,2,784]{3,1,2,0:T(8,128)S(1)}, u32[]{:S(2)}, u32[]{:S(2)}) collective-permute-start(f32[2,8,2,784]{3,1,2,0:T(8,128)S(1)} %fusion.10), channel_id=1, source_target_pairs={{1,0},{2,1},{3,2},{4,3},{5,4},{6,5},{7,6},{0,7},{9,8},{10,9},{11,1... | collective-permute-start | bytes 301064 | tf_op jit(solution)/shard_map/ppermute | solution.py:36
  93.7 2.0 gather_fusion
  97.0 1.1 convolution_bitcast_fusion.1
  98.6 1.7 copy.384
  100.3 5.2 %add_reduce_fusion = (f32[16,4,14,14]{0,3,2,1:T(8,128)S(1)}, f32[16,4,14,14]{0,3,2,1:T(8,128)S(1)}) fusion(f32[16,4,14,2,14,2]{0,5,4,3,2,1:T(2,128)} %bitcast.418, f32[16,4,14,2,14,2]{0,5,4,3,2,1:T(2,128)S(1)} %bitcast.417, f32[16,4,2,2]{0,3,2,1:T(2,128)S(1)} %get-tuple-element.252, f32[16,4,2,2]{0,3,2,1:T(2,128)S(1)} %get-tuple-element.251), kind=kLoop, calls=%fused_computation.4 | loop fusion | flops 376320 | bytes 503808 | tf_op jit(solution)/shard_map/reduce_sum | solution.py:106
  114.8 0.8 subtract_bitcast_fusion.35
  119.8 0.8 subtract_bitcast_fusion.34
  124.8 0.8 subtract_bitcast_fusion.33
  130.4 1.9 fusion.69
  132.3 1.9 collective-permute-start.10
  134.2 5.8 %collective-permute-start.11 = (f32[2,16,3,64]{3,1,2,0:T(8,128)S(1)}, f32[2,16,3,64]{3,1,2,0:T(8,128)S(1)}, u32[]{:S(2)}, u32[]{:S(2)}) collective-permute-start(f32[2,16,3,64]{3,1,2,0:T(8,128)S(1)} %get-tuple-element.166), channel_id=1, source_target_pairs={{1,0},{2,1},{3,2},{4,3},{5,4},{6,5},{7,6},{0,7},{9,8},{10,9},{11,1... | collective-permute-start | bytes 73736 | tf_op jit(solution)/shard_map/ppermute | solution.py:36
  140.1 1.0 fusion.29
  141.9 1.5 multiply_subtract_fusion
  145.3 1.5 gather_fusion.1
  150.3 40.4 %reduce-scatter.2.cloned.1.call-done = f32[2,128,32]{1,2,0:T(8,128)} async-done(((f32[2,128,256]{1,2,0:T(8,128)}), f32[2,128,32]{1,2,0:T(8,128)}) %reduce-scatter.2.cloned.1.call-update) | async-done | bytes 32784 | tf_op jit(solution)/shard_map/reduce_scatter | solution.py:258
  190.7 1.4 fusion.71
  (364 shorter events, 59.5 us)
Async XLA Ops:
  6.5 25.5 %copy-start = (f32[40,2,16,4]{0,3,2,1:T(4,128)S(1)}, f32[40,2,16,4]{0,3,2,1:T(4,128)}, u32[]{:S(2)}) copy-start(f32[40,2,16,4]{0,3,2,1:T(4,128)} %param.13) | copy-start | bytes 61444
  6.5 184.1 %reduce-scatter.2.cloned.1.call-start = ((), (), s32[]{:S(2)}) async-start(), calls=%async_computation.1 | async-start | bytes 294912 | tf_op jit(solution)/shard_map/reduce_scatter | solution.py:258
  8.5 33.5 %copy-start.14 = (pred[256]{0:T(512)(128)(4,1)}, pred[256]{0:T(512)(128)(4,1)S(1)}, u32[]{:S(2)}) copy-start(pred[256]{0:T(512)(128)(4,1)S(1)} %iota_compare_fusion) | copy-start | bytes 772
  17.2 44.1 %collective-permute-start.5 = (bf16[2,128,6,6]{1,0,3,2:T(2,128)(2,1)S(1)}, bf16[2,128,6,6]{1,0,3,2:T(2,128)(2,1)S(1)}, u32[]{:S(2)}, u32[]{:S(2)}) collective-permute-start(bf16[2,128,6,6]{1,0,3,2:T(2,128)(2,1)S(1)} %get-tuple-element.159), channel_id=1, source_target_pairs={{56,0},{64,8},{72,16},{80,24},{88,32},{96,40},{104,48},{112,56},{1... | collective-permute-start | bytes 55304 | tf_op jit(solution)/shard_map/ppermute | solution.py:24
  18.5 44.7 %collective-permute-start.2 = (bf16[2,128,6,6]{1,0,3,2:T(2,128)(2,1)S(1)}, bf16[2,128,6,6]{1,0,3,2:T(2,128)(2,1)S(1)}, u32[]{:S(2)}, u32[]{:S(2)}) collective-permute-start(bf16[2,128,6,6]{1,0,3,2:T(2,128)(2,1)S(1)} %get-tuple-element.160), channel_id=1, source_target_pairs={{0,56},{8,64},{16,72},{24,80},{32,88},{40,96},{48,104},{56,112},{6... | collective-permute-start | bytes 55304 | tf_op jit(solution)/shard_map/ppermute | solution.py:24
  23.7 44.1 %collective-permute-start = (bf16[2,128,6,6]{1,0,3,2:T(2,128)(2,1)S(1)}, bf16[2,128,6,6]{1,0,3,2:T(2,128)(2,1)S(1)}, u32[]{:S(2)}, u32[]{:S(2)}) collective-permute-start(bf16[2,128,6,6]{1,0,3,2:T(2,128)(2,1)S(1)} %get-tuple-element.157), channel_id=1, source_target_pairs={{0,72},{8,80},{16,88},{24,96},{32,104},{40,112},{48,120},{56,128},... | collective-permute-start | bytes 55304 | tf_op jit(solution)/shard_map/ppermute | solution.py:24
  25.9 43.3 %collective-permute-start.7 = (bf16[2,128,6,6]{1,0,3,2:T(2,128)(2,1)S(1)}, bf16[2,128,6,6]{1,0,3,2:T(2,128)(2,1)S(1)}, u32[]{:S(2)}, u32[]{:S(2)}) collective-permute-start(bf16[2,128,6,6]{1,0,3,2:T(2,128)(2,1)S(1)} %get-tuple-element.158), channel_id=1, source_target_pairs={{72,0},{80,8},{88,16},{96,24},{104,32},{112,40},{120,48},{128,56},... | collective-permute-start | bytes 55304 | tf_op jit(solution)/shard_map/ppermute | solution.py:24
  27.2 42.0 %collective-permute-start.4 = (bf16[2,128,16,6]{1,0,3,2:T(2,128)(2,1)S(1)}, bf16[2,128,16,6]{1,0,3,2:T(2,128)(2,1)S(1)}, u32[]{:S(2)}, u32[]{:S(2)}) collective-permute-start(bf16[2,128,16,6]{1,0,3,2:T(2,128)(2,1)S(1)} %get-tuple-element.164), channel_id=1, source_target_pairs={{8,0},{16,8},{24,16},{32,24},{40,32},{48,40},{56,48},{64,56},{72,6... | collective-permute-start | bytes 147464 | tf_op jit(solution)/shard_map/ppermute | solution.py:24
  31.8 64.4 %copy-start.4 = (f32[16]{0:T(128)}, f32[16]{0:T(128)S(1)}, u32[]{:S(2)}) copy-start(f32[16]{0:T(128)S(1)} %get-tuple-element.321) | copy-start | bytes 196
  31.8 64.4 %copy-start.6 = (f32[16]{0:T(128)}, f32[16]{0:T(128)S(1)}, u32[]{:S(2)}) copy-start(f32[16]{0:T(128)S(1)} %get-tuple-element.322) | copy-start | bytes 196
  31.8 64.4 %copy-start.8 = (f32[16]{0:T(128)}, f32[16]{0:T(128)S(1)}, u32[]{:S(2)}) copy-start(f32[16]{0:T(128)S(1)} %get-tuple-element.323) | copy-start | bytes 196
  31.8 64.4 %copy-start.10 = (f32[16]{0:T(128)}, f32[16]{0:T(128)S(1)}, u32[]{:S(2)}) copy-start(f32[16]{0:T(128)S(1)} %get-tuple-element.324) | copy-start | bytes 196
  31.9 64.4 %copy-start.12 = (s32[16]{0:T(128)}, s32[16]{0:T(128)S(1)}, u32[]{:S(2)}) copy-start(s32[16]{0:T(128)S(1)} %add_clamp_fusion) | copy-start | bytes 196
  37.4 23.4 %copy-start.19 = (pred[64]{0:T(512)(128)(4,1)}, pred[64]{0:T(512)(128)(4,1)S(1)}, u32[]{:S(2)}) copy-start(pred[64]{0:T(512)(128)(4,1)S(1)} %and.1081) | copy-start | bytes 196
  37.5 23.4 %copy-start.20 = (pred[64]{0:T(512)(128)(4,1)}, pred[64]{0:T(512)(128)(4,1)S(1)}, u32[]{:S(2)}) copy-start(pred[64]{0:T(512)(128)(4,1)S(1)} %and.1085) | copy-start | bytes 196
  37.6 23.3 %copy-start.21 = (pred[64]{0:T(512)(128)(4,1)}, pred[64]{0:T(512)(128)(4,1)S(1)}, u32[]{:S(2)}) copy-start(pred[64]{0:T(512)(128)(4,1)S(1)} %and.1107) | copy-start | bytes 196
  37.8 23.2 %copy-start.22 = (pred[64]{0:T(512)(128)(4,1)}, pred[64]{0:T(512)(128)(4,1)S(1)}, u32[]{:S(2)}) copy-start(pred[64]{0:T(512)(128)(4,1)S(1)} %and.1111) | copy-start | bytes 196
  37.9 23.1 %copy-start.23 = (pred[64]{0:T(512)(128)(4,1)}, pred[64]{0:T(512)(128)(4,1)S(1)}, u32[]{:S(2)}) copy-start(pred[64]{0:T(512)(128)(4,1)S(1)} %and.1091) | copy-start | bytes 196
  38.0 9.0 %copy-start.24 = (pred[64]{0:T(512)(128)(4,1)}, pred[64]{0:T(512)(128)(4,1)S(1)}, u32[]{:S(2)}) copy-start(pred[64]{0:T(512)(128)(4,1)S(1)} %and.1103) | copy-start | bytes 196
  38.4 8.7 %copy-start.25 = (pred[64]{0:T(512)(128)(4,1)}, pred[64]{0:T(512)(128)(4,1)S(1)}, u32[]{:S(2)}) copy-start(pred[64]{0:T(512)(128)(4,1)S(1)} %and.1134) | copy-start | bytes 196
  38.5 8.7 %copy-start.26 = (pred[64]{0:T(512)(128)(4,1)}, pred[64]{0:T(512)(128)(4,1)S(1)}, u32[]{:S(2)}) copy-start(pred[64]{0:T(512)(128)(4,1)S(1)} %and.1143) | copy-start | bytes 196
  61.3 8.0 %collective-permute-start.3 = (bf16[2,128,16,6]{1,0,3,2:T(2,128)(2,1)S(1)}, bf16[2,128,16,6]{1,0,3,2:T(2,128)(2,1)S(1)}, u32[]{:S(2)}, u32[]{:S(2)}) collective-permute-start(bf16[2,128,16,6]{1,0,3,2:T(2,128)(2,1)S(1)} %get-tuple-element.163), channel_id=1, source_target_pairs={{0,8},{8,16},{16,24},{24,32},{32,40},{40,48},{48,56},{56,64},{64,7... | collective-permute-start | bytes 147464 | tf_op jit(solution)/shard_map/ppermute | solution.py:24
  63.3 6.6 %collective-permute-start.1 = (bf16[2,128,6,16]{1,0,3,2:T(2,128)(2,1)S(1)}, bf16[2,128,6,16]{1,0,3,2:T(2,128)(2,1)S(1)}, u32[]{:S(2)}, u32[]{:S(2)}) collective-permute-start(bf16[2,128,6,16]{1,0,3,2:T(2,128)(2,1)S(1)} %get-tuple-element.161), channel_id=1, source_target_pairs={{0,64},{8,72},{16,80},{24,88},{32,96},{40,104},{48,112},{56,120},{... | collective-permute-start | bytes 147464 | tf_op jit(solution)/shard_map/ppermute | solution.py:24
  67.8 6.6 %collective-permute-start.6 = (bf16[2,128,6,16]{1,0,3,2:T(2,128)(2,1)S(1)}, bf16[2,128,6,16]{1,0,3,2:T(2,128)(2,1)S(1)}, u32[]{:S(2)}, u32[]{:S(2)}) collective-permute-start(bf16[2,128,6,16]{1,0,3,2:T(2,128)(2,1)S(1)} %get-tuple-element.162), channel_id=1, source_target_pairs={{64,0},{72,8},{80,16},{88,24},{96,32},{104,40},{112,48},{120,56},{... | collective-permute-start | bytes 147464 | tf_op jit(solution)/shard_map/ppermute | solution.py:24
  80.6 15.1 %collective-permute-start.8 = (f32[2,8,2,784]{3,1,2,0:T(8,128)S(1)}, f32[2,8,2,784]{3,1,2,0:T(8,128)S(1)}, u32[]{:S(2)}, u32[]{:S(2)}) collective-permute-start(f32[2,8,2,784]{3,1,2,0:T(8,128)S(1)} %fusion.10), channel_id=1, source_target_pairs={{0,1},{1,2},{2,3},{3,4},{4,5},{5,6},{6,7},{7,0},{8,9},{9,10},{10,1... | collective-permute-start | bytes 301064 | tf_op jit(solution)/shard_map/ppermute | solution.py:33
  84.9 11.3 %collective-permute-start.9 = (f32[2,8,2,784]{3,1,2,0:T(8,128)S(1)}, f32[2,8,2,784]{3,1,2,0:T(8,128)S(1)}, u32[]{:S(2)}, u32[]{:S(2)}) collective-permute-start(f32[2,8,2,784]{3,1,2,0:T(8,128)S(1)} %fusion.10), channel_id=1, source_target_pairs={{1,0},{2,1},{3,2},{4,3},{5,4},{6,5},{7,6},{0,7},{9,8},{10,9},{11,1... | collective-permute-start | bytes 301064 | tf_op jit(solution)/shard_map/ppermute | solution.py:36
  130.3 9.8 %copy-start.17 = (pred[288]{0:T(512)(128)(4,1)S(1)}, pred[288]{0:T(512)(128)(4,1)}, u32[]{:S(2)}) copy-start(pred[288]{0:T(512)(128)(4,1)} %compare_and_fusion.1) | copy-start | bytes 868
  132.3 9.7 %copy-start.2 = (f32[16,10,2,2]{0,3,2,1:T(2,128)S(1)}, f32[16,10,2,2]{0,3,2,1:T(2,128)}, u32[]{:S(2)}) copy-start(f32[16,10,2,2]{0,3,2,1:T(2,128)} %get-tuple-element.249) | copy-start | bytes 7684
  132.3 9.7 %copy-start.3 = (f32[16,10,2,2]{0,3,2,1:T(2,128)S(1)}, f32[16,10,2,2]{0,3,2,1:T(2,128)}, u32[]{:S(2)}) copy-start(f32[16,10,2,2]{0,3,2,1:T(2,128)} %get-tuple-element.250) | copy-start | bytes 7684
  132.3 8.8 %collective-permute-start.10 = (f32[2,16,3,64]{3,1,2,0:T(8,128)S(1)}, f32[2,16,3,64]{3,1,2,0:T(8,128)S(1)}, u32[]{:S(2)}, u32[]{:S(2)}) collective-permute-start(f32[2,16,3,64]{3,1,2,0:T(8,128)S(1)} %get-tuple-element.165), channel_id=1, source_target_pairs={{0,1},{1,2},{2,3},{3,4},{4,5},{5,6},{6,7},{7,0},{8,9},{9,10},{10,1... | collective-permute-start | bytes 73736 | tf_op jit(solution)/shard_map/ppermute | solution.py:33
  134.2 7.3 %collective-permute-start.11 = (f32[2,16,3,64]{3,1,2,0:T(8,128)S(1)}, f32[2,16,3,64]{3,1,2,0:T(8,128)S(1)}, u32[]{:S(2)}, u32[]{:S(2)}) collective-permute-start(f32[2,16,3,64]{3,1,2,0:T(8,128)S(1)} %get-tuple-element.166), channel_id=1, source_target_pairs={{1,0},{2,1},{3,2},{4,3},{5,4},{6,5},{7,6},{0,7},{9,8},{10,9},{11,1... | collective-permute-start | bytes 73736 | tf_op jit(solution)/shard_map/ppermute | solution.py:36
  148.3 42.3 %copy-start.32 = (pred[32]{0:T(512)(128)(4,1)S(1)}, pred[32]{0:T(512)(128)(4,1)}, u32[]{:S(2)}) copy-start(pred[32]{0:T(512)(128)(4,1)} %dynamic_slice.12) | copy-start | bytes 100
  (15 other events, 26.8 us)
Sparse Core Ops, SparseCore 0:
  149.2 41.4 reduce-scatter.1
where the time goes:
time: 200 us; the launch traced here: 199 us
  local copies, waits for them, and re-layouts  60.4 us (30%)
  waiting for transfers between devices  46.5 us (23%)
  starting transfers between devices  42.8 us (21%)
  other arithmetic  29.2 us (15%)
  between operations  15.3 us (8%)
  matrix products  4.81 us (2%)
    reduce_scatter x1, waiting for transfers between devices, on_device(): far = lax.psum_scatter(partial_far, 'dir', scatter_dimension=2, tiled=True)  40.4 us
    ppermute x8, starting transfers between devices, shifted(): return lax.ppermute(x, axis, pairs)  22 us
    another operation x80, local copies, waits for them, and re-layouts, translate(): total = total + jnp.where(keep, jnp.stack([real_part, imaginary]), 0.0)  20.8 us
    ppermute x2, starting transfers between devices, padded(): lax.ppermute(lax.slice_in_dim(block, 0, width, axis=dim), axis, backward)  14.6 us
    slice x43, local copies, waits for them, and re-layouts, translate(): op_real = translation[number, 0][:, :, None, None]  10.1 us
    slice x42, local copies, waits for them, and re-layouts, translate(): op_imag = translation[number, 1][:, :, None, None]  10 us
    scatter x1, local copies, waits for them, and re-layouts, on_device(): jnp.zeros_like(currents).at[:, :, cell].set(masked)  7.17 us
    ppermute x2, starting transfers between devices, padded(): lax.ppermute(lax.slice_in_dim(block, block.shape[dim] - width, None, axis...  6.2 us
  transfers between devices with their start and end apart: 13, of which 5 were waited for; matrix products, arithmetic and copies ran while one was open for 17% of the time, Pallas kernels for 0%

commit v1 on v0

v1 whole, which is shorter than its diff:
```python
import functools
import math

import jax
import jax.numpy as jnp
import ml_dtypes
import numpy as np
from jax import lax
from jax.experimental import pallas as pl
from jax.experimental.pallas import tpu as pltpu
from jax.sharding import PartitionSpec as P

U = 128
NT0 = 8
NP0 = 16
NT1 = 16
NP1 = 32
BSIDE = 16
PSIDE = 8
CELLS = 256
GROUPS = 8
QL = NP1 // GROUPS
SAMPLES = NT1 * QL
OWN = CELLS // GROUPS
STRIP = 16
DISP = 40
MESH = pl.DeviceIdType.MESH
F32 = jnp.float32
BF16 = jnp.bfloat16

FIELD_SENDS = (
    (1, 0, 1, 0),
    (-1, 0, 0, 1),
    (0, 1, 3, 2),
    (0, -1, 2, 3),
    (1, 1, 1, 4),
    (1, -1, 1, 5),
    (-1, 1, 0, 6),
    (-1, -1, 0, 7),
)


def lagrange(offset, node):
    first = -(offset - 1.0) * (offset - 2.0) * (offset - 3.0) / 6.0
    second = offset * (offset - 2.0) * (offset - 3.0) / 2.0
    third = -offset * (offset - 1.0) * (offset - 3.0) / 2.0
    fourth = offset * (offset - 1.0) * (offset - 2.0) / 6.0
    return (
        np.where(node == 0, first, 0.0)
        + np.where(node == 1, second, 0.0)
        + np.where(node == 2, third, 0.0)
        + np.where(node == 3, fourth, 0.0)
    )


def weight_tables():
    coarse = np.arange(NT1)[:, None]
    twice = 2 * coarse - 1
    base = np.clip(twice // 4 - 1, 0, NT0 - 4)
    theta = lagrange((twice - 4 * base) / 4.0, np.arange(NT0)[None, :] - base)
    coarse = np.arange(NP1)[:, None]
    twice = 2 * coarse - 1
    base = twice // 4 - 1
    phi = lagrange((twice - 4 * base) / 4.0, (np.arange(NP0)[None, :] - base) % NP0)
    return theta, phi


def halves(x):
    high = x.astype(ml_dtypes.bfloat16)
    low = (x - high.astype(np.float64)).astype(ml_dtypes.bfloat16)
    return high, low


def make_tables():
    theta, phi = weight_tables()
    polar = (np.arange(NT1) + 0.5) * math.pi / NT1
    azimuth = (np.arange(NP1) + 0.5) * 2.0 * math.pi / NP1
    mixed = np.zeros((GROUPS, 128, 128 + 512), ml_dtypes.bfloat16)
    phase = np.zeros((GROUPS, SAMPLES, 128), np.float32)
    for g in range(GROUPS):
        own = np.arange(g * QL, (g + 1) * QL)
        fold = np.einsum("it,qp->iqtp", theta, phi[own]).reshape(SAMPLES, NT0 * NP0)
        mixed[g, :, :128] = np.concatenate(halves(fold), axis=0)
        along_column = np.sin(polar)[:, None] * np.cos(azimuth[own])[None, :]
        along_row = np.sin(polar)[:, None] * np.sin(azimuth[own])[None, :]
        down = np.zeros((2, NT1, QL, 4, 2, NT0, QL))
        for child in range(4):
            oy, ox = child // 2, child % 2
            psi = math.pi * (along_column * (ox - 0.5) + along_row * (oy - 0.5))
            if child < 2:
                phase[g, :, 2 * child] = np.cos(psi).reshape(-1)
                phase[g, :, 2 * child + 1] = np.sin(psi).reshape(-1)
            for q in range(QL):
                real = 0.25 * theta * np.cos(psi[:, q])[:, None]
                imag = 0.25 * theta * np.sin(psi[:, q])[:, None]
                down[0, :, q, child, 0, :, q] = real
                down[1, :, q, child, 0, :, q] = -imag
                down[0, :, q, child, 1, :, q] = imag
                down[1, :, q, child, 1, :, q] = real
        mixed[g, :, 128:] = np.concatenate(halves(down.reshape(128, 256)), axis=1)
    back = np.zeros((GROUPS, 2, 2, NT0, QL, 2, NT0, NP0))
    for g in range(GROUPS):
        for part in range(2):
            for t in range(NT0):
                back[g, :, part, t, :, part, t, :] = phi[g * QL : (g + 1) * QL]
    back = back.reshape(GROUPS * 128, 256).astype(ml_dtypes.bfloat16)
    return mixed, phase, back


def split(x):
    high = x.astype(BF16)
    low = (x - high.astype(F32)).astype(BF16)
    return high, low


def iota(shape, dim):
    return lax.broadcasted_iota(jnp.int32, shape, dim)


def dot(a, b):
    return jnp.dot(a, b, preferred_element_type=F32)


def dot_nt(a, b):
    return lax.dot_general(a, b, (((1,), (1,)), ((), ())), preferred_element_type=F32)


def displacements():
    return [
        (dy, dx) for dy in range(-3, 4) for dx in range(-3, 4) if max(abs(dy), abs(dx)) >= 2
    ]


def kernel(
    across,
    code_ref,
    count_ref,
    cur_hbm,
    rad_hbm,
    near_hbm,
    trans_hbm,
    mixed_hbm,
    phase_hbm,
    back_hbm,
    out_ref,
    cur,
    rad,
    near,
    trans,
    mixed,
    phase,
    back,
    strips,
    fld,
    ext,
    index_col,
    ta,
    tb,
    radm,
    outbox,
    inbox,
    load_sem,
    fs_sem,
    fr_sem,
    ps_sem,
    pr_sem,
    zs_sem,
    zr_sem,
):
    block = lax.axis_index("box")
    group = lax.axis_index("dir")
    row = block // across
    col = block % across

    def neighbour(dr, dc):
        to_row = lax.rem(row + dr + across, across)
        to_col = lax.rem(col + dc + across, across)
        return (to_row * across + to_col, group)

    def peer(step):
        return (block, lax.rem(group + step, GROUPS))

    loads = []
    for number, (source, target) in enumerate(
        (
            (cur_hbm, cur),
            (rad_hbm, rad),
            (mixed_hbm.at[group], mixed),
            (phase_hbm.at[group], phase),
            (trans_hbm, trans),
            (near_hbm, near),
            (back_hbm, back),
        )
    ):
        copy = pltpu.make_async_copy(source, target, load_sem.at[number])
        copy.start()
        loads.append(copy)
    barrier = pltpu.get_barrier_semaphore()
    for dr, dc, _, _ in FIELD_SENDS:
        pl.semaphore_signal(barrier, inc=1, device_id=neighbour(dr, dc), device_id_type=MESH)
    for step in range(1, GROUPS):
        pl.semaphore_signal(barrier, inc=1, device_id=peer(step), device_id_type=MESH)

    code = code_ref[...]
    across_c = ((code >> 2) & 1) + ((code >> 4) & 1) * 2 + ((code >> 6) & 1) * 4
    down_r = ((code >> 3) & 1) + ((code >> 5) & 1) * 2 + ((code >> 7) & 1) * 4
    index_row = (code & 3) * 64 + down_r * 8 + across_c
    live_index = jnp.where(iota((1, CELLS), 1) < count_ref[0], index_row, -1)
    line = iota((64, CELLS), 0)
    kind = line // 16
    a, b = (line % 16) // 8, line % 8
    wanted = jnp.where(
        kind == 0,
        a * 64 + b,
        jnp.where(
            kind == 1,
            184 + a * 64 + b,
            jnp.where(kind == 2, a * 128 + b * 8, 71 + a * 128 + b * 8),
        ),
    )
    rows_wanted = jnp.concatenate([iota((CELLS, CELLS), 0), wanted], axis=0)
    place = jnp.where(rows_wanted == live_index, 1.0, 0.0).astype(BF16)
    loads[0].wait()
    placed = dot_nt(place, cur[...]).astype(BF16)
    fld[0:CELLS, :] = placed[:CELLS]
    strips[...] = placed[CELLS:]

    loads[1].wait()
    loads[2].wait()
    fold = mixed[:, 0:128]
    rr = dot(fold, rad[0:128, :])
    ri = dot(fold, rad[128:256, :])
    rr = rr[:64] + rr[64:]
    ri = ri[:64] + ri[64:]

    pl.semaphore_wait(barrier, len(FIELD_SENDS) + GROUPS - 1)
    sends = []
    for number, (dr, dc, which, slot) in enumerate(FIELD_SENDS):
        copy = pltpu.make_async_remote_copy(
            src_ref=strips.at[pl.ds(which * STRIP, STRIP)],
            dst_ref=fld.at[pl.ds(CELLS + slot * STRIP, STRIP)],
            send_sem=fs_sem.at[number],
            recv_sem=fr_sem.at[slot],
            device_id=neighbour(dr, dc),
            device_id_type=MESH,
        )
        copy.start()
        sends.append(copy)

    loads[3].wait()
    total = jnp.zeros((64, 256), F32)
    for pair in range(2):
        cosine = phase[:, 2 * pair : 2 * pair + 1]
        sine = phase[:, 2 * pair + 1 : 2 * pair + 2]
        cr, ci, sr, si = cosine * rr, cosine * ri, sine * rr, sine * ri
        for child, ar, ai in ((pair, cr + si, ci - sr), (3 - pair, cr - si, ci + sr)):
            arh, arl = split(ar)
            aih, ail = split(ai)
            matrix = jnp.concatenate(
                [
                    jnp.concatenate([arh, -aih], axis=1),
                    jnp.concatenate([aih, arh], axis=1),
                    jnp.concatenate([arl, -ail], axis=1),
                    jnp.concatenate([ail, arl], axis=1),
                ],
                axis=0,
            )
            total = total + dot_nt(placed[child * 64 : (child + 1) * 64], matrix)
    own_parent = total[:, :128] + total[:, 128:]
    ext[3:11, 8:16, :] = own_parent.reshape(PSIDE, PSIDE, 128)

    whole = (pl.ds(3, 8), pl.ds(8, 8))
    parent_sends = (
        (0, 1, whole, (pl.ds(3, 8), pl.ds(0, 8))),
        (0, -1, whole, (pl.ds(3, 8), pl.ds(16, 8))),
        (1, 0, (pl.ds(8, 3), pl.ds(8, 8)), (pl.ds(0, 3), pl.ds(8, 8))),
        (-1, 0, (pl.ds(3, 3), pl.ds(8, 8)), (pl.ds(11, 3), pl.ds(8, 8))),
        (1, 1, (pl.ds(8, 3), pl.ds(8, 8)), (pl.ds(0, 3), pl.ds(0, 8))),
        (1, -1, (pl.ds(8, 3), pl.ds(8, 8)), (pl.ds(0, 3), pl.ds(16, 8))),
        (-1, 1, (pl.ds(3, 3), pl.ds(8, 8)), (pl.ds(11, 3), pl.ds(0, 8))),
        (-1, -1, (pl.ds(3, 3), pl.ds(8, 8)), (pl.ds(11, 3), pl.ds(16, 8))),
    )
    parents = []
    for number, (dr, dc, source, target) in enumerate(parent_sends):
        copy = pltpu.make_async_remote_copy(
            src_ref=ext.at[source[0], source[1]],
            dst_ref=ext.at[target[0], target[1]],
            send_sem=ps_sem.at[number],
            recv_sem=pr_sem.at[number],
            device_id=neighbour(dr, dc),
            device_id_type=MESH,
        )
        copy.start()
        parents.append(copy)

    index_col[...] = jnp.transpose(jnp.broadcast_to(index_row, (128, CELLS)))
    by_slot = index_col[...]
    pick = jnp.concatenate(
        [
            jnp.where(by_slot == iota((CELLS, 128), 1) + first, 1.0, 0.0).astype(BF16)
            for first in (0, 128)
        ],
        axis=1,
    )
    loads[4].wait()
    by_disp = jnp.transpose(trans[...])
    turned = pltpu.roll(by_disp, 64, 1)
    left = iota((DISP, 128), 1) < 64
    ta[...] = jnp.where(left, by_disp, turned)
    tb[...] = jnp.where(left, turned, -by_disp)

    rad_real, rad_imag = rad[0:128, :], rad[128:256, :]
    radm[0:128, 0:128] = rad_real
    radm[0:128, 128:256] = -rad_imag
    radm[128:256, 0:128] = rad_imag
    radm[128:256, 128:256] = rad_real

    own_index = index_col[pl.ds(pl.multiple_of(group * OWN, OWN), OWN), :]
    own_r = ((own_index >> 3) & 7) * 2 + (own_index >> 7)
    own_c = (own_index & 7) * 2 + ((own_index >> 6) & 1)
    edge_n, edge_s = row == 0, row == across - 1
    edge_w, edge_e = col == 0, col == across - 1
    hot = []
    for dr in (-1, 0, 1):
        for dc in (-1, 0, 1):
            r, c = own_r + dr, own_c + dc
            rw, cw = r & 15, c & 15
            by_c = (cw & 1) * 8 + (cw >> 1)
            by_r = (rw & 1) * 8 + (rw >> 1)
            inside = ((rw & 1) * 2 + (cw & 1)) * 64 + (rw >> 1) * 8 + (cw >> 1)
            up, down, west, east = r < 0, r > 15, c < 0, c > 15
            at = jnp.where(west, 256 + 32 + by_r, jnp.where(east, 256 + 48 + by_r, inside))
            at = jnp.where(up, 256 + by_c + jnp.where(west, 64, jnp.where(east, 80, 0)), at)
            at = jnp.where(down, 256 + by_c + jnp.where(west, 96, jnp.where(east, 112, 16)), at)
            gone = (up & edge_n) | (down & edge_s) | (west & edge_w) | (east & edge_e)
            at = jnp.where(gone, -1, at)
            hot.append(
                jnp.concatenate(
                    [
                        jnp.where(at == iota((OWN, 128), 1) + first, 1.0, 0.0).astype(BF16)
                        for first in (0, 128, 256)
                    ],
                    axis=1,
                )
            )
    hot = jnp.concatenate(hot, axis=0)
    for copy in sends:
        copy.wait()
    around = dot(hot, fld[...]).astype(BF16)
    loads[5].wait()
    close = jnp.zeros((2 * OWN, 256), F32)
    for number in range(9):
        mine = around[number * OWN : (number + 1) * OWN]
        stacked = jnp.concatenate([mine[:, :128], mine[:, 128:]], axis=0)
        close = close + dot_nt(stacked, near[pl.ds(number * 256, 256), :])

    for copy in parents:
        copy.wait()

    @pl.when(edge_n)
    def _():
        ext[0:3] = jnp.zeros((3, 24, 128), F32)

    @pl.when(edge_s)
    def _():
        ext[11:14] = jnp.zeros((3, 24, 128), F32)

    @pl.when(edge_w)
    def _():
        ext[:, 0:8, :] = jnp.zeros((14, 8, 128), F32)

    @pl.when(edge_e)
    def _():
        ext[:, 16:24, :] = jnp.zeros((14, 8, 128), F32)

    numbers = {pair: number for number, pair in enumerate(displacements())}
    first = [jnp.zeros((4, PSIDE, 128), F32) for _ in range(2)]
    second = [jnp.zeros((4, PSIDE, 128), F32) for _ in range(2)]
    odd_column = (iota((7, 2, PSIDE, 128), 2) & 1) == 1
    for dx in range(-3, 4):
        tile = ext[:, 8 + dx : 16 + dx, :].reshape(7, 2, PSIDE, 128)
        if dx == -3:
            tile = jnp.where(odd_column, tile, 0.0)
        if dx == 3:
            tile = jnp.where(odd_column, 0.0, tile)
        for dy in range(-3, 4):
            if (dy, dx) not in numbers:
                continue
            number = numbers[dy, dx]
            wa = ta[number : number + 1, :].reshape(1, 1, 128)
            wb = tb[number : number + 1, :].reshape(1, 1, 128)
            for parity in range(2):
                if dy == (-3 if parity == 0 else 3):
                    continue
                start = 3 + dy + parity
                source = tile[start // 2 : start // 2 + 4, start % 2]
                first[parity] = first[parity] + wa * source
                second[parity] = second[parity] + wb * source
    first = jnp.stack(first, axis=1).reshape(64, 128)
    second = jnp.stack(second, axis=1).reshape(64, 128)
    incoming = first + pltpu.roll(second, 64, 1)

    high, low = split(incoming)
    wide = dot(jnp.concatenate([high, low], axis=0), mixed[:, 128:640])
    wide = wide[:64] + wide[64:]
    wide = wide[:, :256] + wide[:, 256:]
    left = iota((64, 128), 1) < 64
    pieces = []
    for pair in range(2):
        here = wide[:, pair * 128 : (pair + 1) * 128]
        turned = pltpu.roll(here, 64, 1)
        for value in (jnp.where(left, here, turned), jnp.where(left, turned, here)):
            top = value.astype(BF16).astype(F32)
            pieces.append(jnp.where(left, top, value - top).astype(BF16))
    chosen = dot(pick, jnp.concatenate(pieces, axis=0)).astype(BF16)
    outbox[...] = chosen.reshape(GROUPS, OWN, 128)

    posts = []
    for step in range(1, GROUPS):
        target = peer(step)
        copy = pltpu.make_async_remote_copy(
            src_ref=outbox.at[target[1]],
            dst_ref=inbox.at[group],
            send_sem=zs_sem.at[step - 1],
            recv_sem=zr_sem.at[step - 1],
            device_id=target,
            device_id_type=MESH,
        )
        copy.start()
        posts.append(copy)
    inbox[group] = outbox[group]
    loads[6].wait()
    for copy in posts:
        copy.wait()
    gathered = jnp.concatenate([inbox[g] for g in range(GROUPS)], axis=1)
    lower = dot(gathered, back[...])
    high, low = split(lower)
    far = dot(jnp.concatenate([high, low], axis=0), radm[...])
    far = far[:OWN] + far[OWN:]
    live = iota((OWN, 128), 0) + group * OWN < count_ref[0]
    real = far[:, :128] + (close[:OWN, :128] - close[OWN:, 128:])
    imag = far[:, 128:] + (close[OWN:, :128] + close[:OWN, 128:])
    out_ref[0] = jnp.where(live, real, 0.0).astype(BF16)
    out_ref[1] = jnp.where(live, imag, 0.0).astype(BF16)


def on_device(across, tables, currents, box_code, box_count, radiation, near_block, translation):
    mixed, phase, back = tables
    vmem = pl.BlockSpec(memory_space=pltpu.VMEM)
    smem = pl.BlockSpec(memory_space=pltpu.SMEM)
    anywhere = pl.BlockSpec(memory_space=pl.ANY)
    result = pl.pallas_call(
        functools.partial(kernel, across),
        out_shape=jax.ShapeDtypeStruct((2, OWN, U), BF16),
        in_specs=[vmem, smem] + [anywhere] * 7,
        out_specs=vmem,
        scratch_shapes=[
            pltpu.VMEM((256, 256), BF16),
            pltpu.VMEM((256, 128), BF16),
            pltpu.VMEM((9 * 256, 128), BF16),
            pltpu.VMEM((128, DISP), F32),
            pltpu.VMEM((128, 640), BF16),
            pltpu.VMEM((SAMPLES, 128), F32),
            pltpu.VMEM((GROUPS * 128, 256), BF16),
            pltpu.VMEM((4 * STRIP, 256), BF16),
            pltpu.VMEM((CELLS + 8 * STRIP, 256), BF16),
            pltpu.VMEM((14, 24, 128), F32),
            pltpu.VMEM((CELLS, 128), jnp.int32),
            pltpu.VMEM((DISP, 128), F32),
            pltpu.VMEM((DISP, 128), F32),
            pltpu.VMEM((256, 256), BF16),
            pltpu.VMEM((GROUPS, OWN, 128), BF16),
            pltpu.VMEM((GROUPS, OWN, 128), BF16),
            pltpu.SemaphoreType.DMA((7,)),
            pltpu.SemaphoreType.DMA((8,)),
            pltpu.SemaphoreType.DMA((8,)),
            pltpu.SemaphoreType.DMA((8,)),
            pltpu.SemaphoreType.DMA((8,)),
            pltpu.SemaphoreType.DMA((7,)),
            pltpu.SemaphoreType.DMA((7,)),
        ],
        compiler_params=pltpu.CompilerParams(
            collective_id=0, has_side_effects=True, vmem_limit_bytes=48 * 1024 * 1024
        ),
    )(
        box_code.reshape(1, CELLS),
        box_count,
        currents.reshape(2 * U, CELLS),
        radiation.reshape(2 * 128, U),
        near_block.reshape(9 * 2 * U, U),
        jnp.transpose(translation, (1, 2, 3, 0)).reshape(128, DISP),
        jnp.asarray(mixed),
        jnp.asarray(phase),
        jnp.asarray(back),
    )
    return jnp.transpose(result, (0, 2, 1))


def solution(mesh):
    across = math.isqrt(mesh.shape["box"])
    tables = make_tables()

    def step(*arrays):
        return on_device(across, tables, *arrays)

    placed = (P(None, None, "box"), P("box"), P("box"), P(), P(), P(None, None, None, "dir"))
    return jax.shard_map(
        step,
        mesh=mesh,
        in_specs=placed,
        out_specs=P(None, None, ("box", "dir")),
        check_vma=False,
    )
```

time: 200 us -> 34.3 us (0.17)
  the two profiles are of different devices: /device:TPU:4 before, /device:TPU:1 now
where the time goes in v1:
time: 34.3 us; the launch traced here: 33.9 us
  Pallas kernels  24.9 us (73%)
  local copies, waits for them, and re-layouts  8.23 us (24%)
  between operations  0.68 us (2%)
    pallas_call x1, Pallas kernels, on_device(): pl.pallas_call(functools.partial(kernel, across), out_shape=jax.ShapeDtyp...  24.9 us
    unnamed x17, local copies, waits for them, and re-layouts  8.23 us

profile of v1, /device:TPU:1, one launch (start us, length us, event | category | flops | bytes accessed | tf_op | source)
XLA Modules:
  0.0 33.9 jit_solution(1355642539746526408)
XLA Ops:
  0.7 0.0 copy-start
  0.7 1.3 %copy-done = bf16[8,128,640]{2,1,0:T(8,128)(2,1)S(1)} copy-done((bf16[8,128,640]{2,1,0:T(8,128)(2,1)S(1)}, bf16[8,128,640]{2,1,0:T(8,128)(2,1)}, u32[]{:S(2)}) %copy-start) | copy-done | bytes 1310744
  2.0 0.0 copy-start.1
  2.0 1.1 %copy-done.1 = bf16[9,2,128,128]{3,2,1,0:T(8,128)(2,1)S(1)} copy-done((bf16[9,2,128,128]{3,2,1,0:T(8,128)(2,1)S(1)}, bf16[9,2,128,128]{3,2,1,0:T(8,128)(2,1)}, u32[]{:S(2)}) %copy-start.1) | copy-done | bytes 589848
  3.0 0.0 copy-start.2
  3.0 1.0 %copy-done.2 = bf16[1024,256]{1,0:T(8,128)(2,1)S(1)} copy-done((bf16[1024,256]{1,0:T(8,128)(2,1)S(1)}, bf16[1024,256]{1,0:T(8,128)(2,1)}, u32[]{:S(2)}) %copy-start.2) | copy-done | bytes 524312
  4.1 0.0 copy-start.3
  4.1 0.9 %copy-done.3 = f32[8,64,128]{2,1,0:T(8,128)S(1)} copy-done((f32[8,64,128]{2,1,0:T(8,128)S(1)}, f32[8,64,128]{2,1,0:T(8,128)}, u32[]{:S(2)}) %copy-start.3) | copy-done | bytes 262168
  5.0 0.0 copy-start.4
  5.0 0.9 %copy-done.4 = bf16[2,128,256]{2,1,0:T(8,128)(2,1)S(1)} copy-done((bf16[2,128,256]{2,1,0:T(8,128)(2,1)S(1)}, bf16[2,128,256]{2,1,0:T(8,128)(2,1)}, u32[]{:S(2)}) %copy-start.4) | copy-done | bytes 131096
  5.9 0.0 copy-start.5
  5.9 0.8 %copy-done.5 = bf16[2,128,128]{2,1,0:T(8,128)(2,1)S(1)} copy-done((bf16[2,128,128]{2,1,0:T(8,128)(2,1)S(1)}, bf16[2,128,128]{2,1,0:T(8,128)(2,1)}, u32[]{:S(2)}) %copy-start.5) | copy-done | bytes 65560
  6.8 0.0 copy-start.6
  6.8 0.8 %copy-done.6 = f32[40,2,16,4]{0,3,2,1:T(4,128)S(1)} copy-done((f32[40,2,16,4]{0,3,2,1:T(4,128)S(1)}, f32[40,2,16,4]{0,3,2,1:T(4,128)}, u32[]{:S(2)}) %copy-start.6) | copy-done | bytes 20504
  7.6 0.0 copy-start.7
  7.6 0.7 %copy-done.7 = s32[256]{0:T(256)S(1)} copy-done((s32[256]{0:T(256)S(1)}, s32[256]{0:T(256)}, u32[]{:S(2)}) %copy-start.7) | copy-done | bytes 1048
  8.3 24.9 %shard_map.91 = bf16[2,32,128]{2,1,0:T(8,128)(2,1)S(1)} custom-call(s32[1,256]{1,0:T(1,128)S(1)} %bitcast.13, s32[1]{0:T(128)S(6)} %copy.11.count_ref, bf16[256,256]{1,0:T(8,128)(2,1)S(1)} %bitcast.9, bf16[256,128]{1,0:T(8,128)(2,1)S(1)} %bitcast.11, bf16[2304,128]{1,0:T(8,128)(2,1)S(1)} %bitcast.8, f32[128,40]{1,0:T(8,128)S(1)} %bitcast.12, ...), custom_call_target="tpu_custom_call" | custom-call | tf_op jit(solution)/shard_map/pallas_call | solution.py:452
  33.2 0.6 %copy.12 = bf16[2,128,32]{1,2,0:T(8,128)(2,1)} copy(bf16[2,128,32]{1,2,0:T(8,128)(2,1)S(1)} %bitcast.10) | data formatting | bytes 32768
Async XLA Ops:
  0.7 1.3 %copy-start = (bf16[8,128,640]{2,1,0:T(8,128)(2,1)S(1)}, bf16[8,128,640]{2,1,0:T(8,128)(2,1)}, u32[]{:S(2)}) copy-start(bf16[8,128,640]{2,1,0:T(8,128)(2,1)} %constant.6.clone.mixed_hbm) | copy-start | bytes 3932164
  2.0 1.1 %copy-start.1 = (bf16[9,2,128,128]{3,2,1,0:T(8,128)(2,1)S(1)}, bf16[9,2,128,128]{3,2,1,0:T(8,128)(2,1)}, u32[]{:S(2)}) copy-start(bf16[9,2,128,128]{3,2,1,0:T(8,128)(2,1)} %param.13) | copy-start | bytes 1769476
  3.0 1.0 %copy-start.2 = (bf16[1024,256]{1,0:T(8,128)(2,1)S(1)}, bf16[1024,256]{1,0:T(8,128)(2,1)}, u32[]{:S(2)}) copy-start(bf16[1024,256]{1,0:T(8,128)(2,1)} %constant.8.clone.back_hbm) | copy-start | bytes 1572868
  4.1 0.9 %copy-start.3 = (f32[8,64,128]{2,1,0:T(8,128)S(1)}, f32[8,64,128]{2,1,0:T(8,128)}, u32[]{:S(2)}) copy-start(f32[8,64,128]{2,1,0:T(8,128)} %constant.7.clone.phase_hbm) | copy-start | bytes 786436
  5.0 0.9 %copy-start.4 = (bf16[2,128,256]{2,1,0:T(8,128)(2,1)S(1)}, bf16[2,128,256]{2,1,0:T(8,128)(2,1)}, u32[]{:S(2)}) copy-start(bf16[2,128,256]{2,1,0:T(8,128)(2,1)} %param.9) | copy-start | bytes 393220
  5.9 0.8 %copy-start.5 = (bf16[2,128,128]{2,1,0:T(8,128)(2,1)S(1)}, bf16[2,128,128]{2,1,0:T(8,128)(2,1)}, u32[]{:S(2)}) copy-start(bf16[2,128,128]{2,1,0:T(8,128)(2,1)} %param.12) | copy-start | bytes 196612
  6.8 0.8 %copy-start.6 = (f32[40,2,16,4]{0,3,2,1:T(4,128)S(1)}, f32[40,2,16,4]{0,3,2,1:T(4,128)}, u32[]{:S(2)}) copy-start(f32[40,2,16,4]{0,3,2,1:T(4,128)} %param.14) | copy-start | bytes 61444
  7.6 0.7 %copy-start.7 = (s32[256]{0:T(256)S(1)}, s32[256]{0:T(256)}, u32[]{:S(2)}) copy-start(s32[256]{0:T(256)} %param.10) | copy-start | bytes 3076

commit v2 on v1

--- a/solution.py
+++ b/solution.py
@@ -133,7 +133,7 @@
 
 def kernel(
     across,
-    code_ref,
+    code_hbm,
     count_ref,
     cur_hbm,
     rad_hbm,
@@ -143,6 +143,7 @@
     phase_hbm,
     back_hbm,
     out_ref,
+    code_ref,
     cur,
     rad,
     near,
@@ -190,6 +191,7 @@
             (trans_hbm, trans),
             (near_hbm, near),
             (back_hbm, back),
+            (code_hbm, code_ref),
         )
     ):
         copy = pltpu.make_async_copy(source, target, load_sem.at[number])
@@ -201,6 +203,7 @@
     for step in range(1, GROUPS):
         pl.semaphore_signal(barrier, inc=1, device_id=peer(step), device_id_type=MESH)
 
+    loads[7].wait()
     code = code_ref[...]
     across_c = ((code >> 2) & 1) + ((code >> 4) & 1) * 2 + ((code >> 6) & 1) * 4
     down_r = ((code >> 3) & 1) + ((code >> 5) & 1) * 2 + ((code >> 7) & 1) * 4
@@ -224,7 +227,6 @@
     placed = dot_nt(place, cur[...]).astype(BF16)
     fld[0:CELLS, :] = placed[:CELLS]
     strips[...] = placed[CELLS:]
-
     loads[1].wait()
     loads[2].wait()
     fold = mixed[:, 0:128]
@@ -268,7 +270,6 @@
             total = total + dot_nt(placed[child * 64 : (child + 1) * 64], matrix)
     own_parent = total[:, :128] + total[:, 128:]
     ext[3:11, 8:16, :] = own_parent.reshape(PSIDE, PSIDE, 128)
-
     whole = (pl.ds(3, 8), pl.ds(8, 8))
     parent_sends = (
         (0, 1, whole, (pl.ds(3, 8), pl.ds(0, 8))),
@@ -353,7 +354,6 @@
         mine = around[number * OWN : (number + 1) * OWN]
         stacked = jnp.concatenate([mine[:, :128], mine[:, 128:]], axis=0)
         close = close + dot_nt(stacked, near[pl.ds(number * 256, 256), :])
-
     for copy in parents:
         copy.wait()
 
@@ -399,7 +399,6 @@
     first = jnp.stack(first, axis=1).reshape(64, 128)
     second = jnp.stack(second, axis=1).reshape(64, 128)
     incoming = first + pltpu.roll(second, 64, 1)
-
     high, low = split(incoming)
     wide = dot(jnp.concatenate([high, low], axis=0), mixed[:, 128:640])
     wide = wide[:64] + wide[64:]
@@ -414,7 +413,6 @@
             pieces.append(jnp.where(left, top, value - top).astype(BF16))
     chosen = dot(pick, jnp.concatenate(pieces, axis=0)).astype(BF16)
     outbox[...] = chosen.reshape(GROUPS, OWN, 128)
-
     posts = []
     for step in range(1, GROUPS):
         target = peer(step)
@@ -446,15 +444,26 @@
 
 def on_device(across, tables, currents, box_code, box_count, radiation, near_block, translation):
     mixed, phase, back = tables
+    operands = (
+        box_code.reshape(1, CELLS),
+        box_count,
+        currents.reshape(2 * U, CELLS),
+        radiation.reshape(2 * 128, U),
+        near_block.reshape(9 * 2 * U, U),
+        jnp.transpose(translation, (1, 2, 3, 0)).reshape(128, DISP),
+        jnp.asarray(mixed),
+        jnp.asarray(phase),
+        jnp.asarray(back),
+    )
     vmem = pl.BlockSpec(memory_space=pltpu.VMEM)
-    smem = pl.BlockSpec(memory_space=pltpu.SMEM)
-    anywhere = pl.BlockSpec(memory_space=pl.ANY)
+    outside = pl.BlockSpec(memory_space=pltpu.HBM)
     result = pl.pallas_call(
         functools.partial(kernel, across),
         out_shape=jax.ShapeDtypeStruct((2, OWN, U), BF16),
-        in_specs=[vmem, smem] + [anywhere] * 7,
+        in_specs=[outside, pl.BlockSpec(memory_space=pltpu.SMEM)] + [outside] * 7,
         out_specs=vmem,
         scratch_shapes=[
+            pltpu.VMEM((1, CELLS), jnp.int32),
             pltpu.VMEM((256, 256), BF16),
             pltpu.VMEM((256, 128), BF16),
             pltpu.VMEM((9 * 256, 128), BF16),
@@ -471,7 +480,7 @@
             pltpu.VMEM((256, 256), BF16),
             pltpu.VMEM((GROUPS, OWN, 128), BF16),
             pltpu.VMEM((GROUPS, OWN, 128), BF16),
-            pltpu.SemaphoreType.DMA((7,)),
+            pltpu.SemaphoreType.DMA((8,)),
             pltpu.SemaphoreType.DMA((8,)),
             pltpu.SemaphoreType.DMA((8,)),
             pltpu.SemaphoreType.DMA((8,)),
@@ -482,17 +491,7 @@
         compiler_params=pltpu.CompilerParams(
             collective_id=0, has_side_effects=True, vmem_limit_bytes=48 * 1024 * 1024
         ),
-    )(
-        box_code.reshape(1, CELLS),
-        box_count,
-        currents.reshape(2 * U, CELLS),
-        radiation.reshape(2 * 128, U),
-        near_block.reshape(9 * 2 * U, U),
-        jnp.transpose(translation, (1, 2, 3, 0)).reshape(128, DISP),
-        jnp.asarray(mixed),
-        jnp.asarray(phase),
-        jnp.asarray(back),
-    )
+    )(*(pltpu.with_memory_space_constraint(x, pltpu.HBM) if x.size > 1 else x for x in operands))
     return jnp.transpose(result, (0, 2, 1))
 
 

time: 34.3 us -> 25.6 us (0.75)
  local copies, waits for them, and re-layouts: 8.23 us -> 0.61 us
  Pallas kernels: 24.9 us -> 24.2 us
    unnamed x17 -> x1, local copies, waits for them, and re-layouts: 8.23 us -> 0.61 us
    pallas_call x1, Pallas kernels: 24.9 us -> 24.2 us  [on_device(): pl.pallas_call(functools.partial(kernel, across), out_shape=jax.ShapeDtyp...]
where the time goes in v2:
time: 25.6 us; the launch traced here: 25.5 us
  Pallas kernels  24.2 us (95%)
  between operations  0.66 us (3%)
  local copies, waits for them, and re-layouts  0.61 us (2%)
    pallas_call x1, Pallas kernels, on_device(): pl.pallas_call(functools.partial(kernel, across), out_shape=jax.ShapeDtyp...  24.2 us
    unnamed x1, local copies, waits for them, and re-layouts  0.61 us

profile of v2, /device:TPU:1, one launch (start us, length us, event | category | flops | bytes accessed | tf_op | source)
XLA Modules:
  0.0 25.5 jit_solution(5949872092640113328)
XLA Ops:
  0.7 24.2 %shard_map.91 = bf16[2,32,128]{2,1,0:T(8,128)(2,1)S(1)} custom-call(s32[1,256]{1,0:T(1,128)} %bitcast.13, s32[1]{0:T(128)S(6)} %copy.11.count_ref, bf16[256,256]{1,0:T(8,128)(2,1)} %bitcast.10, bf16[256,128]{1,0:T(8,128)(2,1)} %bitcast.11, bf16[2304,128]{1,0:T(8,128)(2,1)} %bitcast.9, f32[128,40]{1,0:T(8,128)} %bitcast.12, ...), custom_call_target="tpu_custom_call" | custom-call | tf_op jit(solution)/shard_map/pallas_call | solution.py:460
  24.9 0.6 %copy.12 = bf16[2,128,32]{1,2,0:T(8,128)(2,1)} copy(bf16[2,128,32]{1,2,0:T(8,128)(2,1)S(1)} %bitcast.8) | data formatting | bytes 32768

commit v3 on v0

v3 whole, which is shorter than its diff:
```python
import functools
import math

import jax
import jax.numpy as jnp
import ml_dtypes
import numpy as np
from jax import lax
from jax.experimental import pallas as pl
from jax.experimental.pallas import tpu as pltpu
from jax.sharding import PartitionSpec as P

U = 128
NT0 = 8
NP0 = 16
NT1 = 16
NP1 = 32
PSIDE = 8
CELLS = 256
GROUPS = 8
QL = NP1 // GROUPS
SAMPLES = NT1 * QL
OWN = CELLS // GROUPS
DISP = 40
STAGE = 4
MESH = pl.DeviceIdType.MESH
F32 = jnp.float32
BF16 = jnp.bfloat16

STEPS = ((1, 0), (-1, 0), (0, 1), (0, -1), (1, 1), (-1, -1), (1, -1), (-1, 1))
PIECES = (
    ("own", 32, 32, 64),
    ("own", 0, 32, 96),
    ("side", 32, 32, 128),
    ("side", 0, 32, 160),
    ("side", 48, 16, 192),
    ("side", 0, 16, 240),
    ("side", 16, 16, 208),
    ("side", 32, 16, 224),
)


def lagrange(offset, node):
    first = -(offset - 1.0) * (offset - 2.0) * (offset - 3.0) / 6.0
    second = offset * (offset - 2.0) * (offset - 3.0) / 2.0
    third = -offset * (offset - 1.0) * (offset - 3.0) / 2.0
    fourth = offset * (offset - 1.0) * (offset - 2.0) / 6.0
    return (
        np.where(node == 0, first, 0.0)
        + np.where(node == 1, second, 0.0)
        + np.where(node == 2, third, 0.0)
        + np.where(node == 3, fourth, 0.0)
    )


def make_tables():
    coarse = np.arange(NT1)[:, None]
    twice = 2 * coarse - 1
    base = np.clip(twice // 4 - 1, 0, NT0 - 4)
    theta = lagrange((twice - 4 * base) / 4.0, np.arange(NT0)[None, :] - base)
    coarse = np.arange(NP1)[:, None]
    twice = 2 * coarse - 1
    base = twice // 4 - 1
    phi = lagrange((twice - 4 * base) / 4.0, (np.arange(NP0)[None, :] - base) % NP0)
    polar = (np.arange(NT1) + 0.5) * math.pi / NT1
    azimuth = (np.arange(NP1) + 0.5) * 2.0 * math.pi / NP1
    fold = np.zeros((GROUPS, 2 * SAMPLES, NT0 * NP0), ml_dtypes.bfloat16)
    phase = np.zeros((GROUPS, SAMPLES, 128), np.float32)
    for g in range(GROUPS):
        own = np.arange(g * QL, (g + 1) * QL)
        full = np.einsum("it,qp->iqtp", theta, phi[own]).reshape(SAMPLES, NT0 * NP0)
        high = full.astype(ml_dtypes.bfloat16)
        fold[g, :SAMPLES] = high
        fold[g, SAMPLES:] = (full - high.astype(np.float64)).astype(ml_dtypes.bfloat16)
        along_column = np.sin(polar)[:, None] * np.cos(azimuth[own])[None, :]
        along_row = np.sin(polar)[:, None] * np.sin(azimuth[own])[None, :]
        for child in range(2):
            psi = math.pi * (along_column * (child - 0.5) - along_row * 0.5)
            phase[g, :, 2 * child] = np.cos(psi).reshape(-1)
            phase[g, :, 2 * child + 1] = np.sin(psi).reshape(-1)
    return fold, phase


def split(x):
    high = x.astype(BF16)
    low = (x - high.astype(F32)).astype(BF16)
    return high, low


def iota(shape, dim):
    return lax.broadcasted_iota(jnp.int32, shape, dim)


def dot(a, b):
    return jnp.dot(a, b, preferred_element_type=F32)


def dot_nt(a, b):
    return lax.dot_general(a, b, (((1,), (1,)), ((), ())), preferred_element_type=F32)


def displacements():
    return [
        (dy, dx) for dy in range(-3, 4) for dx in range(-3, 4) if max(abs(dy), abs(dx)) >= 2
    ]


def translated(parents, ta, tb):
    numbers = {pair: number for number, pair in enumerate(displacements())}
    first = [jnp.zeros((4, PSIDE, 128), F32) for _ in range(2)]
    second = [jnp.zeros((4, PSIDE, 128), F32) for _ in range(2)]
    odd_column = (iota((8, 2, PSIDE, 128), 2) & 1) == 1
    for dx in range(-3, 4):
        tile = parents[:, 8 + dx : 16 + dx, :].reshape(8, 2, PSIDE, 128)
        if dx == -3:
            tile = jnp.where(odd_column, tile, 0.0)
        if dx == 3:
            tile = jnp.where(odd_column, 0.0, tile)
        for dy in range(-3, 4):
            if (dy, dx) not in numbers:
                continue
            number = numbers[dy, dx]
            wa = ta[number : number + 1, :].reshape(1, 1, 128)
            wb = tb[number : number + 1, :].reshape(1, 1, 128)
            for parity in range(2):
                if dy == (-3 if parity == 0 else 3):
                    continue
                start = 4 + dy + parity
                source = tile[start // 2 : start // 2 + 4, start % 2]
                first[parity] = first[parity] + wa * source
                second[parity] = second[parity] + wb * source
    first = jnp.stack(first, axis=1).reshape(64, 128)
    second = jnp.stack(second, axis=1).reshape(64, 128)
    return first + pltpu.roll(second, 64, 1)


def kernel(
    across,
    code_hbm,
    count_ref,
    cur_hbm,
    rad_hbm,
    near_hbm,
    trans_hbm,
    fold_hbm,
    phase_hbm,
    out_ref,
    code_ref,
    cur,
    rad,
    near,
    trans,
    fold,
    phase,
    ops,
    ta,
    tb,
    field,
    side,
    mats,
    ext,
    index_col,
    load_sem,
    fs_sem,
    fr_sem,
    ts_sem,
    tr_sem,
    next_sem,
    above_sem,
):
    block = lax.axis_index("box")
    group = lax.axis_index("dir")
    row = block // across
    col = block % across

    loads = []
    for number, (source, target) in enumerate(
        (
            (trans_hbm, trans),
            (code_hbm, code_ref),
            (cur_hbm, cur),
            (rad_hbm, rad),
            (fold_hbm, fold),
            (phase_hbm, phase),
            (near_hbm, near),
        )
    ):
        copy = pltpu.make_async_copy(source, target, load_sem.at[number])
        copy.start()
        loads.append(copy)

    def rank(r, c):
        return jnp.where(2 * r < across, r, 3 * across // 2 - 1 - r) * across + (c ^ 1)

    def beside(number):
        dr, dc = STEPS[number]
        r, c = row + dr, col + dc
        there = (r >= 0) & (r < across) & (c >= 0) & (c < across)
        return there, rank(r, c) < rank(row, col), (r * across + c, group)

    def peer(other):
        return (block, other)

    barrier = pltpu.get_barrier_semaphore()
    earlier = group
    for number in range(8):
        there, before, device = beside(number)

        @pl.when(there & jnp.logical_not(before))
        def _():
            pl.semaphore_signal(barrier, inc=1, device_id=device, device_id_type=MESH)

        earlier = earlier + jnp.where(there & before, 1, 0)
    for other in range(GROUPS):

        @pl.when(other > group)
        def _():
            pl.semaphore_signal(barrier, inc=1, device_id=peer(other), device_id_type=MESH)

    loads[0].wait()
    ops[group] = jnp.transpose(trans[...])

    @pl.when(earlier > 0)
    def _():
        pl.semaphore_wait(barrier, earlier)

    def send_ops(other):
        return pltpu.make_async_remote_copy(
            src_ref=ops.at[group],
            dst_ref=ops.at[group],
            send_sem=ts_sem.at[other],
            recv_sem=tr_sem.at[group],
            device_id=peer(other),
            device_id_type=MESH,
        )

    for other in range(GROUPS):

        @pl.when(other < group)
        def _():
            pl.semaphore_signal(
                above_sem.at[group], inc=1, device_id=peer(other), device_id_type=MESH
            )
            send_ops(other).start()

    for number in range(8):
        there, before, device = beside(number)

        @pl.when(there & before)
        def _():
            pl.semaphore_signal(
                next_sem.at[number ^ 1], inc=1, device_id=device, device_id_type=MESH
            )

    loads[1].wait()
    code = code_ref[...]
    across_c = ((code >> 2) & 1) + ((code >> 4) & 1) * 2 + ((code >> 6) & 1) * 4
    down_r = ((code >> 3) & 1) + ((code >> 5) & 1) * 2 + ((code >> 7) & 1) * 4
    index_row = (code & 3) * 64 + down_r * 8 + across_c
    live_index = jnp.where(iota((1, CELLS), 1) < count_ref[0], index_row, -1)
    line = iota((128, CELLS), 0)
    beyond = line - 64
    wanted = jnp.where(
        line < 64, line, ((beyond & 31) >> 2) * 8 + (beyond >> 5) * 4 + (beyond & 3)
    )
    loads[2].wait()
    place = jnp.concatenate(
        [
            jnp.where(wanted == live_index - child * 64, 1.0, 0.0).astype(BF16)
            for child in range(4)
        ],
        axis=0,
    )
    placed = dot_nt(place, cur[...]).astype(BF16).reshape(4, 128, 256)
    field[:, 0:64, :] = placed[:, :64]
    side[...] = placed[:, 64:]

    def send_field(number, device):
        buffer, start, size, target = PIECES[number]
        source = field if buffer == "own" else side
        return pltpu.make_async_remote_copy(
            src_ref=source.at[:, pl.ds(start, size), :],
            dst_ref=field.at[:, pl.ds(target, size), :],
            send_sem=fs_sem.at[number],
            recv_sem=fr_sem.at[number],
            device_id=device,
            device_id_type=MESH,
        )

    for first in (True, False):
        for number in range(8):
            there, before, device = beside(number)

            @pl.when(there & (before if first else jnp.logical_not(before)))
            def _():
                if not first:
                    pl.semaphore_wait(next_sem.at[number], 1)
                send_field(number, device).start()

    for edge, pieces in (
        (row == 0, ((64, 32), (192, 32))),
        (row == across - 1, ((96, 32), (224, 32))),
        (col == 0, ((128, 32), (192, 16), (224, 16))),
        (col == across - 1, ((160, 32), (208, 16), (240, 16))),
    ):

        @pl.when(edge)
        def _():
            for start, size in pieces:
                field[:, start : start + size, :] = jnp.zeros((4, size, 256), BF16)

    loads[3].wait()
    loads[4].wait()
    loads[5].wait()

    def prepare(g, _):
        weights = fold[pl.ds(pl.multiple_of(g * 128, 128), 128), :]
        rr = dot(weights, rad[0:128, :])
        ri = dot(weights, rad[128:256, :])
        rr = rr[:64] + rr[64:]
        ri = ri[:64] + ri[64:]
        turns = phase[g]
        total = jnp.zeros((64, 256), F32)
        for pair in range(2):
            cosine = turns[:, 2 * pair : 2 * pair + 1]
            sine = turns[:, 2 * pair + 1 : 2 * pair + 2]
            cr, ci, sr, si = cosine * rr, cosine * ri, sine * rr, sine * ri
            for child, ar, ai in ((pair, cr + si, ci - sr), (3 - pair, cr - si, ci + sr)):
                arh, arl = split(ar)
                aih, ail = split(ai)
                matrix = jnp.concatenate(
                    [
                        jnp.concatenate([arh, -aih], axis=1),
                        jnp.concatenate([aih, arh], axis=1),
                        jnp.concatenate([arl, -ail], axis=1),
                        jnp.concatenate([ail, arl], axis=1),
                    ],
                    axis=0,
                )
                mats[g, child] = matrix
                total = total + dot_nt(field[child, 0:64, :], matrix)
        total = total[:, :128] + total[:, 128:]
        ext[g, 4:12, 8:16, :] = total.reshape(PSIDE, PSIDE, 128)
        return 0

    lax.fori_loop(0, GROUPS, prepare, 0)

    index_col[...] = jnp.transpose(jnp.broadcast_to(index_row, (128, CELLS)))
    own_index = index_col[pl.ds(pl.multiple_of(group * OWN, OWN), OWN), :]
    pick = jnp.concatenate(
        [
            jnp.where(own_index[:, :64] == iota((OWN, 64), 1) + child * 64, 1.0, 0.0).astype(BF16)
            for child in range(4)
        ],
        axis=0,
    )
    own_r = ((own_index >> 3) & 7) * 2 + (own_index >> 7)
    own_c = (own_index & 7) * 2 + ((own_index >> 6) & 1)
    hot = []
    for dr in (-1, 0, 1):
        for dc in (-1, 0, 1):
            r, c = own_r + dr, own_c + dc
            child = (r & 1) * 2 + (c & 1)
            pr, pc = r >> 1, c >> 1
            north, south, west, east = pr < 0, pr > 7, pc < 0, pc > 7
            at = jnp.where(west, 131 + pr * 4, jnp.where(east, 160 + pr * 4, pr * 8 + pc))
            at = jnp.where(north, jnp.where(west, 207, jnp.where(east, 220, 88 + pc)), at)
            at = jnp.where(south, jnp.where(west, 227, jnp.where(east, 240, 96 + pc)), at)
            at = at + child * 256
            hot.append(
                jnp.concatenate(
                    [
                        jnp.where(at == iota((OWN, 128), 1) + start, 1.0, 0.0).astype(BF16)
                        for start in range(0, 1024, 128)
                    ],
                    axis=1,
                )
            )
    hot = jnp.concatenate(hot, axis=0)

    def send_up():
        for other in range(1, GROUPS):

            @pl.when(other > group)
            def _():
                pl.semaphore_wait(above_sem.at[other], 1)
                send_ops(other).start()

    pl.when(2 * group >= GROUPS)(send_up)
    for number in range(8):
        there, _, device = beside(number ^ 1)

        @pl.when(there)
        def _():
            send_field(number, device).wait_recv()

    around = dot(hot, field[...].reshape(1024, 256)).astype(BF16)
    loads[6].wait()
    close = jnp.zeros((2 * OWN, 256), F32)
    for number in range(9):
        mine = around[number * OWN : (number + 1) * OWN]
        stacked = jnp.concatenate([mine[:, :128], mine[:, 128:]], axis=0)
        close = close + dot_nt(stacked, near[pl.ds(number * 256, 256), :])

    def rim(g, _):
        total = jnp.zeros((192, 256), F32)
        for child in range(4):
            total = total + dot_nt(field[child, 64:256, :], mats[g, child])
        total = total[:, :128] + total[:, 128:]
        ext[g, 0:4, 8:16, :] = total[0:32].reshape(4, 8, 128)
        ext[g, 12:16, 8:16, :] = total[32:64].reshape(4, 8, 128)
        for r in range(8):
            ext[g, 4 + r, 4:8, :] = total[64 + 4 * r : 68 + 4 * r]
            ext[g, 4 + r, 16:20, :] = total[96 + 4 * r : 100 + 4 * r]
        for r in range(4):
            ext[g, r, 4:8, :] = total[128 + 4 * r : 132 + 4 * r]
            ext[g, r, 16:20, :] = total[144 + 4 * r : 148 + 4 * r]
            ext[g, 12 + r, 4:8, :] = total[160 + 4 * r : 164 + 4 * r]
            ext[g, 12 + r, 16:20, :] = total[176 + 4 * r : 180 + 4 * r]
        return 0

    lax.fori_loop(0, GROUPS, rim, 0)
    pl.when(2 * group < GROUPS)(send_up)

    left = iota((DISP, 128), 1) < 64
    far = jnp.zeros((2 * OWN, 256), F32)
    for stage in range(0, GROUPS, STAGE):
        for g in range(stage, stage + STAGE):

            @pl.when(g != group)
            def _():
                pltpu.make_async_remote_copy(
                    src_ref=ops.at[g],
                    dst_ref=ops.at[g],
                    send_sem=ts_sem.at[g],
                    recv_sem=tr_sem.at[g],
                    device_id=peer(g),
                    device_id_type=MESH,
                ).wait_recv()

        for g in range(stage, stage + STAGE):
            here = ops[g]
            turned = pltpu.roll(here, 64, 1)
            ta[g] = jnp.where(left, here, turned)
            tb[g] = jnp.where(left, turned, -here)
            high, low = split(translated(ext.at[g], ta.at[g], tb.at[g]))
            chosen = dot(pick, jnp.concatenate([high, low], axis=1)).astype(BF16)
            for child in range(4):
                mine = chosen[child * OWN : (child + 1) * OWN]
                high, low = mine[:, :128], mine[:, 128:]
                stacked = jnp.concatenate(
                    [
                        jnp.concatenate([high, high], axis=1),
                        jnp.concatenate([low, jnp.zeros_like(low)], axis=1),
                    ],
                    axis=0,
                )
                far = far + dot(stacked, mats[g, child])

    live = iota((OWN, 128), 0) + group * OWN < count_ref[0]
    far = 0.25 * (far[:OWN] + far[OWN:])
    real = far[:, :128] + (close[:OWN, :128] - close[OWN:, 128:])
    imag = far[:, 128:] + (close[OWN:, :128] + close[:OWN, 128:])
    out_ref[0] = jnp.where(live, real, 0.0).astype(BF16)
    out_ref[1] = jnp.where(live, imag, 0.0).astype(BF16)

    for number in range(8):
        there, _, device = beside(number)

        @pl.when(there)
        def _():
            send_field(number, device).wait_send()

    for other in range(GROUPS):

        @pl.when(other != group)
        def _():
            send_ops(other).wait_send()


def on_device(across, tables, currents, box_code, box_count, radiation, near_block, translation):
    fold, phase = tables
    operands = (
        box_code.reshape(1, CELLS),
        box_count,
        currents.reshape(2 * U, CELLS),
        radiation.reshape(2 * 128, U),
        near_block.reshape(9 * 2 * U, U),
        jnp.transpose(translation, (1, 2, 3, 0)).reshape(128, DISP),
        jnp.asarray(fold).reshape(GROUPS * 128, 128),
        jnp.asarray(phase),
    )
    outside = pl.BlockSpec(memory_space=pltpu.HBM)
    result = pl.pallas_call(
        functools.partial(kernel, across),
        out_shape=jax.ShapeDtypeStruct((2, OWN, U), BF16),
        in_specs=[outside, pl.BlockSpec(memory_space=pltpu.SMEM)] + [outside] * 6,
        out_specs=pl.BlockSpec(memory_space=pltpu.VMEM),
        scratch_shapes=[
            pltpu.VMEM((1, CELLS), jnp.int32),
            pltpu.VMEM((256, 256), BF16),
            pltpu.VMEM((256, 128), BF16),
            pltpu.VMEM((9 * 256, 128), BF16),
            pltpu.VMEM((128, DISP), F32),
            pltpu.VMEM((GROUPS * 128, 128), BF16),
            pltpu.VMEM((GROUPS, SAMPLES, 128), F32),
            pltpu.VMEM((GROUPS, DISP, 128), F32),
            pltpu.VMEM((GROUPS, DISP, 128), F32),
            pltpu.VMEM((GROUPS, DISP, 128), F32),
            pltpu.VMEM((4, 256, 256), BF16),
            pltpu.VMEM((4, 64, 256), BF16),
            pltpu.VMEM((GROUPS, 4, 256, 256), BF16),
            pltpu.VMEM((GROUPS, 16, 24, 128), F32),
            pltpu.VMEM((CELLS, 128), jnp.int32),
            pltpu.SemaphoreType.DMA((7,)),
            pltpu.SemaphoreType.DMA((8,)),
            pltpu.SemaphoreType.DMA((8,)),
            pltpu.SemaphoreType.DMA((GROUPS,)),
            pltpu.SemaphoreType.DMA((GROUPS,)),
            pltpu.SemaphoreType.REGULAR((8,)),
            pltpu.SemaphoreType.REGULAR((GROUPS,)),
        ],
        compiler_params=pltpu.CompilerParams(
            collective_id=0, has_side_effects=True, vmem_limit_bytes=48 * 1024 * 1024
        ),
    )(*(pltpu.with_memory_space_constraint(x, pltpu.HBM) if x.size > 1 else x for x in operands))
    return jnp.transpose(result, (0, 2, 1))


def solution(mesh):
    across = math.isqrt(mesh.shape["box"])
    tables = make_tables()

    def step(*arrays):
        return on_device(across, tables, *arrays)

    placed = (P(None, None, "box"), P("box"), P("box"), P(), P(), P(None, None, None, "dir"))
    return jax.shard_map(
        step,
        mesh=mesh,
        in_specs=placed,
        out_specs=P(None, None, ("box", "dir")),
        check_vma=False,
    )
```

time: 200 us -> 22.5 us (0.11)
  the two profiles are of different devices: /device:TPU:4 before, /device:TPU:1 now
where the time goes in v3:
time: 22.5 us; the launch traced here: 22.4 us
  Pallas kernels  21.1 us (94%)
  between operations  0.66 us (3%)
  local copies, waits for them, and re-layouts  0.61 us (3%)
    pallas_call x1, Pallas kernels, on_device(): pl.pallas_call(functools.partial(kernel, across), out_shape=jax.ShapeDtyp...  21.1 us
    unnamed x1, local copies, waits for them, and re-layouts  0.61 us

profile of v3, /device:TPU:1, one launch (start us, length us, event | category | flops | bytes accessed | tf_op | source)
XLA Modules:
  0.0 22.4 jit_solution(15761036423097226486)
XLA Ops:
  0.7 21.1 %shard_map.82 = bf16[2,32,128]{2,1,0:T(8,128)(2,1)S(1)} custom-call(s32[1,256]{1,0:T(1,128)} %bitcast.13, s32[1]{0:T(128)S(6)} %copy.10.count_ref, bf16[256,256]{1,0:T(8,128)(2,1)} %bitcast.10, bf16[256,128]{1,0:T(8,128)(2,1)} %bitcast.11, bf16[2304,128]{1,0:T(8,128)(2,1)} %bitcast.9, f32[128,40]{1,0:T(8,128)} %bitcast.12, ...), custom_call_target="tpu_custom_call" | custom-call | tf_op jit(solution)/shard_map/pallas_call | solution.py:494
  21.7 0.6 %copy.11 = bf16[2,128,32]{1,2,0:T(8,128)(2,1)} copy(bf16[2,128,32]{1,2,0:T(8,128)(2,1)S(1)} %bitcast.8) | data formatting | bytes 32768

commit v4 on v3

--- a/solution.py
+++ b/solution.py
@@ -22,21 +22,21 @@
 SAMPLES = NT1 * QL
 OWN = CELLS // GROUPS
 DISP = 40
-STAGE = 4
+EARLY = 3
 MESH = pl.DeviceIdType.MESH
 F32 = jnp.float32
 BF16 = jnp.bfloat16
 
-STEPS = ((1, 0), (-1, 0), (0, 1), (0, -1), (1, 1), (-1, -1), (1, -1), (-1, 1))
+STEPS = ((1, 1), (-1, -1), (1, -1), (-1, 1), (1, 0), (-1, 0), (0, 1), (0, -1))
 PIECES = (
+    ("side", 48, 16, 192),
+    ("side", 0, 16, 240),
+    ("side", 16, 16, 208),
+    ("side", 32, 16, 224),
     ("own", 32, 32, 64),
     ("own", 0, 32, 96),
     ("side", 32, 32, 128),
     ("side", 0, 32, 160),
-    ("side", 48, 16, 192),
-    ("side", 0, 16, 240),
-    ("side", 16, 16, 208),
-    ("side", 32, 16, 224),
 )
 
 
@@ -66,6 +66,7 @@
     azimuth = (np.arange(NP1) + 0.5) * 2.0 * math.pi / NP1
     fold = np.zeros((GROUPS, 2 * SAMPLES, NT0 * NP0), ml_dtypes.bfloat16)
     phase = np.zeros((GROUPS, SAMPLES, 128), np.float32)
+    turn = np.zeros((GROUPS, 8, 2, SAMPLES), np.float32)
     for g in range(GROUPS):
         own = np.arange(g * QL, (g + 1) * QL)
         full = np.einsum("it,qp->iqtp", theta, phi[own]).reshape(SAMPLES, NT0 * NP0)
@@ -78,7 +79,10 @@
             psi = math.pi * (along_column * (child - 0.5) - along_row * 0.5)
             phase[g, :, 2 * child] = np.cos(psi).reshape(-1)
             phase[g, :, 2 * child + 1] = np.sin(psi).reshape(-1)
-    return fold, phase
+            turn[g, 2 * child] = np.cos(psi).reshape(-1)
+            turn[g, 2 * child + 1, 0] = -np.sin(psi).reshape(-1)
+            turn[g, 2 * child + 1, 1] = np.sin(psi).reshape(-1)
+    return fold, phase, turn
 
 
 def split(x):
@@ -144,6 +148,7 @@
     trans_hbm,
     fold_hbm,
     phase_hbm,
+    turn_hbm,
     out_ref,
     code_ref,
     cur,
@@ -152,12 +157,15 @@
     trans,
     fold,
     phase,
+    turn,
     ops,
     ta,
     tb,
     field,
     side,
     mats,
+    base,
+    found,
     ext,
     index_col,
     load_sem,
@@ -183,11 +191,13 @@
             (fold_hbm, fold),
             (phase_hbm, phase),
             (near_hbm, near),
+            (turn_hbm, turn),
         )
     ):
         copy = pltpu.make_async_copy(source, target, load_sem.at[number])
-        copy.start()
         loads.append(copy)
+
+    loads[0].start()
 
     def rank(r, c):
         return jnp.where(2 * r < across, r, 3 * across // 2 - 1 - r) * across + (c ^ 1)
@@ -217,12 +227,32 @@
         def _():
             pl.semaphore_signal(barrier, inc=1, device_id=peer(other), device_id_type=MESH)
 
-    loads[0].wait()
-    ops[group] = jnp.transpose(trans[...])
+    for copy in loads[1:]:
+        copy.start()
 
     @pl.when(earlier > 0)
     def _():
         pl.semaphore_wait(barrier, earlier)
+
+    for other in range(GROUPS):
+
+        @pl.when(other < group)
+        def _():
+            pl.semaphore_signal(
+                above_sem.at[group], inc=1, device_id=peer(other), device_id_type=MESH
+            )
+
+    for number in range(8):
+        there, before, device = beside(number)
+
+        @pl.when(there & before)
+        def _():
+            pl.semaphore_signal(
+                next_sem.at[number ^ 1], inc=1, device_id=device, device_id_type=MESH
+            )
+
+    loads[0].wait()
+    ops[group] = jnp.transpose(trans[...])
 
     def send_ops(other):
         return pltpu.make_async_remote_copy(
@@ -238,19 +268,7 @@
 
         @pl.when(other < group)
         def _():
-            pl.semaphore_signal(
-                above_sem.at[group], inc=1, device_id=peer(other), device_id_type=MESH
-            )
             send_ops(other).start()
-
-    for number in range(8):
-        there, before, device = beside(number)
-
-        @pl.when(there & before)
-        def _():
-            pl.semaphore_signal(
-                next_sem.at[number ^ 1], inc=1, device_id=device, device_id_type=MESH
-            )
 
     loads[1].wait()
     code = code_ref[...]
@@ -271,24 +289,25 @@
         ],
         axis=0,
     )
-    placed = dot_nt(place, cur[...]).astype(BF16).reshape(4, 128, 256)
-    field[:, 0:64, :] = placed[:, :64]
-    side[...] = placed[:, 64:]
+    placed = dot_nt(place, cur[...]).astype(BF16)
+    for child in range(4):
+        field[0:64, pl.ds(child * 256, 256)] = placed[child * 128 : child * 128 + 64]
+        side[:, pl.ds(child * 256, 256)] = placed[child * 128 + 64 : child * 128 + 128]
 
     def send_field(number, device):
         buffer, start, size, target = PIECES[number]
         source = field if buffer == "own" else side
         return pltpu.make_async_remote_copy(
-            src_ref=source.at[:, pl.ds(start, size), :],
-            dst_ref=field.at[:, pl.ds(target, size), :],
+            src_ref=source.at[pl.ds(start, size)],
+            dst_ref=field.at[pl.ds(target, size)],
             send_sem=fs_sem.at[number],
             recv_sem=fr_sem.at[number],
             device_id=device,
             device_id_type=MESH,
         )
 
-    for first in (True, False):
-        for number in range(8):
+    def send_fields(numbers, first):
+        for number in numbers:
             there, before, device = beside(number)
 
             @pl.when(there & (before if first else jnp.logical_not(before)))
@@ -296,6 +315,8 @@
                 if not first:
                     pl.semaphore_wait(next_sem.at[number], 1)
                 send_field(number, device).start()
+
+    send_fields(range(8), True)
 
     for edge, pieces in (
         (row == 0, ((64, 32), (192, 32))),
@@ -307,20 +328,24 @@
         @pl.when(edge)
         def _():
             for start, size in pieces:
-                field[:, start : start + size, :] = jnp.zeros((4, size, 256), BF16)
-
+                field[start : start + size, :] = jnp.zeros((size, 1024), BF16)
     loads[3].wait()
     loads[4].wait()
     loads[5].wait()
 
-    def prepare(g, _):
-        weights = fold[pl.ds(pl.multiple_of(g * 128, 128), 128), :]
+    def prepare(g):
+        weights = fold[pl.ds(g * 128, 128), :]
         rr = dot(weights, rad[0:128, :])
         ri = dot(weights, rad[128:256, :])
         rr = rr[:64] + rr[64:]
         ri = ri[:64] + ri[64:]
+        rrh, rrl = split(rr)
+        rih, ril = split(ri)
+        base[pl.ds(g * 256, 64), :] = jnp.concatenate([rrh, -rih], axis=1)
+        base[pl.ds(g * 256 + 64, 64), :] = jnp.concatenate([rih, rrh], axis=1)
+        base[pl.ds(g * 256 + 128, 64), :] = jnp.concatenate([rrl, -ril], axis=1)
+        base[pl.ds(g * 256 + 192, 64), :] = jnp.concatenate([ril, rrl], axis=1)
         turns = phase[g]
-        total = jnp.zeros((64, 256), F32)
         for pair in range(2):
             cosine = turns[:, 2 * pair : 2 * pair + 1]
             sine = turns[:, 2 * pair + 1 : 2 * pair + 2]
@@ -337,23 +362,20 @@
                     ],
                     axis=0,
                 )
-                mats[g, child] = matrix
-                total = total + dot_nt(field[child, 0:64, :], matrix)
+                mats[g, :, pl.ds(child * 256, 256)] = matrix
+        total = dot_nt(field[0:64, :], mats[g])
         total = total[:, :128] + total[:, 128:]
         ext[g, 4:12, 8:16, :] = total.reshape(PSIDE, PSIDE, 128)
-        return 0
-
-    lax.fori_loop(0, GROUPS, prepare, 0)
-
+
+    for g in range(GROUPS):
+        if g == EARLY:
+            send_fields((0, 1, 2, 3, 4, 5), False)
+        prepare(g)
+    send_fields((6, 7), False)
     index_col[...] = jnp.transpose(jnp.broadcast_to(index_row, (128, CELLS)))
     own_index = index_col[pl.ds(pl.multiple_of(group * OWN, OWN), OWN), :]
-    pick = jnp.concatenate(
-        [
-            jnp.where(own_index[:, :64] == iota((OWN, 64), 1) + child * 64, 1.0, 0.0).astype(BF16)
-            for child in range(4)
-        ],
-        axis=0,
-    )
+    pick = jnp.where((own_index[:, :64] & 63) == iota((OWN, 64), 1), 1.0, 0.0).astype(BF16)
+    own_child = own_index >> 6
     own_r = ((own_index >> 3) & 7) * 2 + (own_index >> 7)
     own_c = (own_index & 7) * 2 + ((own_index >> 6) & 1)
     hot = []
@@ -377,7 +399,6 @@
                 )
             )
     hot = jnp.concatenate(hot, axis=0)
-
     def send_up():
         for other in range(1, GROUPS):
 
@@ -386,7 +407,7 @@
                 pl.semaphore_wait(above_sem.at[other], 1)
                 send_ops(other).start()
 
-    pl.when(2 * group >= GROUPS)(send_up)
+    send_up()
     for number in range(8):
         there, _, device = beside(number ^ 1)
 
@@ -394,18 +415,20 @@
         def _():
             send_field(number, device).wait_recv()
 
-    around = dot(hot, field[...].reshape(1024, 256)).astype(BF16)
+    around = jnp.zeros((9 * OWN, 256), F32)
+    for child in range(4):
+        lanes = pl.ds(child * 256, 256)
+        around = around + dot(hot[:, child * 256 : (child + 1) * 256], field[:, lanes])
+    around = around.astype(BF16)
     loads[6].wait()
+    loads[7].wait()
     close = jnp.zeros((2 * OWN, 256), F32)
     for number in range(9):
         mine = around[number * OWN : (number + 1) * OWN]
         stacked = jnp.concatenate([mine[:, :128], mine[:, 128:]], axis=0)
         close = close + dot_nt(stacked, near[pl.ds(number * 256, 256), :])
-
-    def rim(g, _):
-        total = jnp.zeros((192, 256), F32)
-        for child in range(4):
-            total = total + dot_nt(field[child, 64:256, :], mats[g, child])
+    def rim(g):
+        total = dot_nt(field[64:256, :], mats[g])
         total = total[:, :128] + total[:, 128:]
         ext[g, 0:4, 8:16, :] = total[0:32].reshape(4, 8, 128)
         ext[g, 12:16, 8:16, :] = total[32:64].reshape(4, 8, 128)
@@ -417,45 +440,47 @@
             ext[g, r, 16:20, :] = total[144 + 4 * r : 148 + 4 * r]
             ext[g, 12 + r, 4:8, :] = total[160 + 4 * r : 164 + 4 * r]
             ext[g, 12 + r, 16:20, :] = total[176 + 4 * r : 180 + 4 * r]
-        return 0
-
-    lax.fori_loop(0, GROUPS, rim, 0)
-    pl.when(2 * group < GROUPS)(send_up)
-
+
+    for g in range(GROUPS):
+        rim(g)
     left = iota((DISP, 128), 1) < 64
-    far = jnp.zeros((2 * OWN, 256), F32)
-    for stage in range(0, GROUPS, STAGE):
-        for g in range(stage, stage + STAGE):
-
-            @pl.when(g != group)
-            def _():
-                pltpu.make_async_remote_copy(
-                    src_ref=ops.at[g],
-                    dst_ref=ops.at[g],
-                    send_sem=ts_sem.at[g],
-                    recv_sem=tr_sem.at[g],
-                    device_id=peer(g),
-                    device_id_type=MESH,
-                ).wait_recv()
-
-        for g in range(stage, stage + STAGE):
-            here = ops[g]
-            turned = pltpu.roll(here, 64, 1)
-            ta[g] = jnp.where(left, here, turned)
-            tb[g] = jnp.where(left, turned, -here)
-            high, low = split(translated(ext.at[g], ta.at[g], tb.at[g]))
-            chosen = dot(pick, jnp.concatenate([high, low], axis=1)).astype(BF16)
-            for child in range(4):
-                mine = chosen[child * OWN : (child + 1) * OWN]
-                high, low = mine[:, :128], mine[:, 128:]
-                stacked = jnp.concatenate(
-                    [
-                        jnp.concatenate([high, high], axis=1),
-                        jnp.concatenate([low, jnp.zeros_like(low)], axis=1),
-                    ],
-                    axis=0,
-                )
-                far = far + dot(stacked, mats[g, child])
+    for g in range(GROUPS):
+
+        @pl.when(g != group)
+        def _():
+            pltpu.make_async_remote_copy(
+                src_ref=ops.at[g],
+                dst_ref=ops.at[g],
+                send_sem=ts_sem.at[g],
+                recv_sem=tr_sem.at[g],
+                device_id=peer(g),
+                device_id_type=MESH,
+            ).wait_recv()
+
+        here = ops[g]
+        turned = pltpu.roll(here, 64, 1)
+        ta[g] = jnp.where(left, here, turned)
+        tb[g] = jnp.where(left, turned, -here)
+        high, low = split(translated(ext.at[g], ta.at[g], tb.at[g]))
+        found[:, g * 256 : g * 256 + 128] = high
+        found[:, g * 256 + 128 : g * 256 + 256] = low
+
+    chosen = dot(pick, found[...])
+    outer = (own_child == 0) | (own_child == 3)
+    upper = own_child < 2
+    tops, bottoms = [], []
+    for g in range(GROUPS):
+        value = chosen[:, g * 256 : g * 256 + 128] + chosen[:, g * 256 + 128 : g * 256 + 256]
+        cosine = jnp.where(outer, turn[g, 0:1, :], turn[g, 2:3, :])
+        sine = jnp.where(outer, turn[g, 1:2, :], turn[g, 3:4, :])
+        sine = jnp.where(upper, sine, -sine)
+        high, low = split(cosine * value + sine * pltpu.roll(value, 64, 1))
+        tops += [high, high]
+        bottoms += [low, jnp.zeros_like(low)]
+    stacked = jnp.concatenate(
+        [jnp.concatenate(tops, axis=1), jnp.concatenate(bottoms, axis=1)], axis=0
+    )
+    far = dot(stacked, base[...])
 
     live = iota((OWN, 128), 0) + group * OWN < count_ref[0]
     far = 0.25 * (far[:OWN] + far[OWN:])
@@ -479,7 +504,7 @@
 
 
 def on_device(across, tables, currents, box_code, box_count, radiation, near_block, translation):
-    fold, phase = tables
+    fold, phase, turn = tables
     operands = (
         box_code.reshape(1, CELLS),
         box_count,
@@ -489,12 +514,13 @@
         jnp.transpose(translation, (1, 2, 3, 0)).reshape(128, DISP),
         jnp.asarray(fold).reshape(GROUPS * 128, 128),
         jnp.asarray(phase),
+        jnp.asarray(turn).reshape(GROUPS, 8, 128),
     )
     outside = pl.BlockSpec(memory_space=pltpu.HBM)
     result = pl.pallas_call(
         functools.partial(kernel, across),
         out_shape=jax.ShapeDtypeStruct((2, OWN, U), BF16),
-        in_specs=[outside, pl.BlockSpec(memory_space=pltpu.SMEM)] + [outside] * 6,
+        in_specs=[outside, pl.BlockSpec(memory_space=pltpu.SMEM)] + [outside] * 7,
         out_specs=pl.BlockSpec(memory_space=pltpu.VMEM),
         scratch_shapes=[
             pltpu.VMEM((1, CELLS), jnp.int32),
@@ -504,15 +530,18 @@
             pltpu.VMEM((128, DISP), F32),
             pltpu.VMEM((GROUPS * 128, 128), BF16),
             pltpu.VMEM((GROUPS, SAMPLES, 128), F32),
+            pltpu.VMEM((GROUPS, 8, 128), F32),
             pltpu.VMEM((GROUPS, DISP, 128), F32),
             pltpu.VMEM((GROUPS, DISP, 128), F32),
             pltpu.VMEM((GROUPS, DISP, 128), F32),
-            pltpu.VMEM((4, 256, 256), BF16),
-            pltpu.VMEM((4, 64, 256), BF16),
-            pltpu.VMEM((GROUPS, 4, 256, 256), BF16),
+            pltpu.VMEM((256, 1024), BF16),
+            pltpu.VMEM((64, 1024), BF16),
+            pltpu.VMEM((GROUPS, 256, 1024), BF16),
+            pltpu.VMEM((GROUPS * 256, 256), BF16),
+            pltpu.VMEM((64, GROUPS * 256), BF16),
             pltpu.VMEM((GROUPS, 16, 24, 128), F32),
             pltpu.VMEM((CELLS, 128), jnp.int32),
-            pltpu.SemaphoreType.DMA((7,)),
+            pltpu.SemaphoreType.DMA((8,)),
             pltpu.SemaphoreType.DMA((8,)),
             pltpu.SemaphoreType.DMA((8,)),
             pltpu.SemaphoreType.DMA((GROUPS,)),

time: 22.5 us -> 19.4 us (0.86)
  Pallas kernels: 21.1 us -> 18 us
    pallas_call x1, Pallas kernels: 21.1 us -> 18 us  [on_device(): pl.pallas_call(functools.partial(kernel, across), out_shape=jax.ShapeDtyp...]
where the time goes in v4:
time: 19.4 us; the launch traced here: 19.2 us
  Pallas kernels  18 us (93%)
  between operations  0.66 us (3%)
  local copies, waits for them, and re-layouts  0.61 us (3%)
    pallas_call x1, Pallas kernels, on_device(): pl.pallas_call(functools.partial(kernel, across), out_shape=jax.ShapeDtyp...  18 us
    unnamed x1, local copies, waits for them, and re-layouts  0.61 us

profile of v4, /device:TPU:1, one launch (start us, length us, event | category | flops | bytes accessed | tf_op | source)
XLA Modules:
  0.0 19.2 jit_solution(3549445821731484370)
XLA Ops:
  0.7 18.0 %shard_map.91 = bf16[2,32,128]{2,1,0:T(8,128)(2,1)S(1)} custom-call(s32[1,256]{1,0:T(1,128)} %bitcast.13, s32[1]{0:T(128)S(6)} %copy.11.count_ref, bf16[256,256]{1,0:T(8,128)(2,1)} %bitcast.10, bf16[256,128]{1,0:T(8,128)(2,1)} %bitcast.11, bf16[2304,128]{1,0:T(8,128)(2,1)} %bitcast.9, f32[128,40]{1,0:T(8,128)} %bitcast.12, ...), custom_call_target="tpu_custom_call" | custom-call | tf_op jit(solution)/shard_map/pallas_call | solution.py:520
  18.6 0.6 %copy.12 = bf16[2,128,32]{1,2,0:T(8,128)(2,1)} copy(bf16[2,128,32]{1,2,0:T(8,128)(2,1)S(1)} %bitcast.8) | data formatting | bytes 32768

commit v5 on v4

--- a/solution.py
+++ b/solution.py
@@ -200,7 +200,8 @@
     loads[0].start()
 
     def rank(r, c):
-        return jnp.where(2 * r < across, r, 3 * across // 2 - 1 - r) * across + (c ^ 1)
+        usual = jnp.where(2 * r < across, r, 3 * across // 2 - 1 - r) * across + (c ^ 1)
+        return jnp.where((group == 0) & (r == 0) & (c == 0), across * across, usual)
 
     def beside(number):
         dr, dc = STEPS[number]

time: 19.4 us -> 18 us (0.928)
  the two profiles are of different devices: /device:TPU:1 before, /device:TPU:35 now
where the time goes in v5:
time: 18 us; the launch traced here: 17.8 us
  Pallas kernels  16.6 us (92%)
  between operations  0.66 us (4%)
  local copies, waits for them, and re-layouts  0.61 us (3%)
    pallas_call x1, Pallas kernels, on_device(): pl.pallas_call(functools.partial(kernel, across), out_shape=jax.ShapeDtyp...  16.6 us
    unnamed x1, local copies, waits for them, and re-layouts  0.61 us

profile of v5, /device:TPU:35, one launch (start us, length us, event | category | flops | bytes accessed | tf_op | source)
XLA Modules:
  0.0 17.8 jit_solution(14195091395210089333)
XLA Ops:
  0.7 16.6 %shard_map.91 = bf16[2,32,128]{2,1,0:T(8,128)(2,1)S(1)} custom-call(s32[1,256]{1,0:T(1,128)} %bitcast.13, s32[1]{0:T(128)S(6)} %copy.11.count_ref, bf16[256,256]{1,0:T(8,128)(2,1)} %bitcast.10, bf16[256,128]{1,0:T(8,128)(2,1)} %bitcast.11, bf16[2304,128]{1,0:T(8,128)(2,1)} %bitcast.9, f32[128,40]{1,0:T(8,128)} %bitcast.12, ...), custom_call_target="tpu_custom_call" | custom-call | tf_op jit(solution)/shard_map/pallas_call | solution.py:521
  17.2 0.6 %copy.12 = bf16[2,128,32]{1,2,0:T(8,128)(2,1)} copy(bf16[2,128,32]{1,2,0:T(8,128)(2,1)S(1)} %bitcast.8) | data formatting | bytes 32768

commit v6 on v4

--- a/solution.py
+++ b/solution.py
@@ -22,7 +22,7 @@
 SAMPLES = NT1 * QL
 OWN = CELLS // GROUPS
 DISP = 40
-EARLY = 3
+EARLY = 1
 MESH = pl.DeviceIdType.MESH
 F32 = jnp.float32
 BF16 = jnp.bfloat16
@@ -200,7 +200,9 @@
     loads[0].start()
 
     def rank(r, c):
-        return jnp.where(2 * r < across, r, 3 * across // 2 - 1 - r) * across + (c ^ 1)
+        usual = jnp.where(2 * r < across, 11 * r, 36 + 6 * (across - 1 - r))
+        usual = (usual + 4 * c + 9 - 13 * (c & 1)) * across * across + r * across + c
+        return jnp.where((group == 0) & (r == 0) & (c == 0), 1 << 20, usual)
 
     def beside(number):
         dr, dc = STEPS[number]
@@ -227,7 +229,7 @@
         def _():
             pl.semaphore_signal(barrier, inc=1, device_id=peer(other), device_id_type=MESH)
 
-    for copy in loads[1:]:
+    for copy in loads[1:6]:
         copy.start()
 
     @pl.when(earlier > 0)
@@ -269,6 +271,9 @@
         @pl.when(other < group)
         def _():
             send_ops(other).start()
+
+    for copy in loads[6:]:
+        copy.start()
 
     loads[1].wait()
     code = code_ref[...]
@@ -399,15 +404,20 @@
                 )
             )
     hot = jnp.concatenate(hot, axis=0)
-    def send_up():
-        for other in range(1, GROUPS):
+    def send_up(others):
+        for other in others:
 
             @pl.when(other > group)
             def _():
                 pl.semaphore_wait(above_sem.at[other], 1)
                 send_ops(other).start()
 
-    send_up()
+    send_up(range(1, GROUPS // 2))
+
+    @pl.when(group >= 1)
+    def _():
+        send_up(range(GROUPS // 2, GROUPS))
+
     for number in range(8):
         there, _, device = beside(number ^ 1)
 
@@ -443,6 +453,10 @@
 
     for g in range(GROUPS):
         rim(g)
+    @pl.when(group < 1)
+    def _():
+        send_up(range(GROUPS // 2, GROUPS))
+
     left = iota((DISP, 128), 1) < 64
     for g in range(GROUPS):
 

time: 19.4 us -> 17.8 us (0.918)
  the two profiles are of different devices: /device:TPU:1 before, /device:TPU:10 now
where the time goes in v6:
time: 17.8 us; the launch traced here: 17.7 us
  Pallas kernels  16.4 us (92%)
  between operations  0.66 us (4%)
  local copies, waits for them, and re-layouts  0.61 us (3%)
    pallas_call x1, Pallas kernels, on_device(): pl.pallas_call(functools.partial(kernel, across), out_shape=jax.ShapeDtyp...  16.4 us
    unnamed x1, local copies, waits for them, and re-layouts  0.61 us

profile of v6, /device:TPU:10, one launch (start us, length us, event | category | flops | bytes accessed | tf_op | source)
XLA Modules:
  0.0 17.7 jit_solution(8429541779033736177)
XLA Ops:
  0.7 16.4 %shard_map.91 = bf16[2,32,128]{2,1,0:T(8,128)(2,1)S(1)} custom-call(s32[1,256]{1,0:T(1,128)} %bitcast.13, s32[1]{0:T(128)S(6)} %copy.11.count_ref, bf16[256,256]{1,0:T(8,128)(2,1)} %bitcast.10, bf16[256,128]{1,0:T(8,128)(2,1)} %bitcast.11, bf16[2304,128]{1,0:T(8,128)(2,1)} %bitcast.9, f32[128,40]{1,0:T(8,128)} %bitcast.12, ...), custom_call_target="tpu_custom_call" | custom-call | tf_op jit(solution)/shard_map/pallas_call | solution.py:534
  17.1 0.6 %copy.12 = bf16[2,128,32]{1,2,0:T(8,128)(2,1)} copy(bf16[2,128,32]{1,2,0:T(8,128)(2,1)S(1)} %bitcast.8) | data formatting | bytes 32768

commit v7 on v6

--- a/solution.py
+++ b/solution.py
@@ -311,17 +311,24 @@
             device_id_type=MESH,
         )
 
-    def send_fields(numbers, first):
+    def send_fields(numbers, turn_of):
         for number in numbers:
             there, before, device = beside(number)
-
-            @pl.when(there & (before if first else jnp.logical_not(before)))
+            last = (group == 0) & (device[0] == 0)
+            if turn_of == "before":
+                due = before
+            elif turn_of == "after":
+                due = jnp.logical_not(before | last)
+            else:
+                due = last
+
+            @pl.when(there & due)
             def _():
-                if not first:
+                if turn_of != "before":
                     pl.semaphore_wait(next_sem.at[number], 1)
                 send_field(number, device).start()
 
-    send_fields(range(8), True)
+    send_fields(range(8), "before")
 
     for edge, pieces in (
         (row == 0, ((64, 32), (192, 32))),
@@ -374,9 +381,9 @@
 
     for g in range(GROUPS):
         if g == EARLY:
-            send_fields((0, 1, 2, 3, 4, 5), False)
+            send_fields((0, 1, 2, 3, 4, 5), "after")
         prepare(g)
-    send_fields((6, 7), False)
+    send_fields((6, 7), "after")
     index_col[...] = jnp.transpose(jnp.broadcast_to(index_row, (128, CELLS)))
     own_index = index_col[pl.ds(pl.multiple_of(group * OWN, OWN), OWN), :]
     pick = jnp.where((own_index[:, :64] & 63) == iota((OWN, 64), 1), 1.0, 0.0).astype(BF16)
@@ -418,6 +425,7 @@
     def _():
         send_up(range(GROUPS // 2, GROUPS))
 
+    send_fields(range(8), "last")
     for number in range(8):
         there, _, device = beside(number ^ 1)
 

time: 17.8 us -> 17.7 us (level)
  the two profiles are of different devices: /device:TPU:10 before, /device:TPU:35 now
where the time goes in v7:
time: 17.7 us; the launch traced here: 17.5 us
  Pallas kernels  16.3 us (92%)
  between operations  0.66 us (4%)
  local copies, waits for them, and re-layouts  0.61 us (3%)
    pallas_call x1, Pallas kernels, on_device(): pl.pallas_call(functools.partial(kernel, across), out_shape=jax.ShapeDtyp...  16.3 us
    unnamed x1, local copies, waits for them, and re-layouts  0.61 us

profile of v7, /device:TPU:35, one launch (start us, length us, event | category | flops | bytes accessed | tf_op | source)
XLA Modules:
  0.0 17.5 jit_solution(1290715794648080128)
XLA Ops:
  0.7 16.3 %shard_map.91 = bf16[2,32,128]{2,1,0:T(8,128)(2,1)S(1)} custom-call(s32[1,256]{1,0:T(1,128)} %bitcast.13, s32[1]{0:T(128)S(6)} %copy.11.count_ref, bf16[256,256]{1,0:T(8,128)(2,1)} %bitcast.10, bf16[256,128]{1,0:T(8,128)(2,1)} %bitcast.11, bf16[2304,128]{1,0:T(8,128)(2,1)} %bitcast.9, f32[128,40]{1,0:T(8,128)} %bitcast.12, ...), custom_call_target="tpu_custom_call" | custom-call | tf_op jit(solution)/shard_map/pallas_call | solution.py:542
  16.9 0.6 %copy.12 = bf16[2,128,32]{1,2,0:T(8,128)(2,1)} copy(bf16[2,128,32]{1,2,0:T(8,128)(2,1)S(1)} %bitcast.8) | data formatting | bytes 32768

commit v8 on v7

--- a/solution.py
+++ b/solution.py
@@ -184,7 +184,7 @@
     loads = []
     for number, (source, target) in enumerate(
         (
-            (trans_hbm, trans),
+            (trans_hbm.at[pl.ds(0, 64)], trans.at[pl.ds(0, 64)]),
             (code_hbm, code_ref),
             (cur_hbm, cur),
             (rad_hbm, rad),
@@ -192,12 +192,14 @@
             (phase_hbm, phase),
             (near_hbm, near),
             (turn_hbm, turn),
+            (trans_hbm.at[pl.ds(64, 64)], trans.at[pl.ds(64, 64)]),
         )
     ):
         copy = pltpu.make_async_copy(source, target, load_sem.at[number])
         loads.append(copy)
 
     loads[0].start()
+    loads[8].start()
 
     def rank(r, c):
         usual = jnp.where(2 * r < across, 11 * r, 36 + 6 * (across - 1 - r))
@@ -254,6 +256,7 @@
             )
 
     loads[0].wait()
+    loads[8].wait()
     ops[group] = jnp.transpose(trans[...])
 
     def send_ops(other):
@@ -272,7 +275,7 @@
         def _():
             send_ops(other).start()
 
-    for copy in loads[6:]:
+    for copy in loads[6:8]:
         copy.start()
 
     loads[1].wait()
@@ -563,7 +566,7 @@
             pltpu.VMEM((64, GROUPS * 256), BF16),
             pltpu.VMEM((GROUPS, 16, 24, 128), F32),
             pltpu.VMEM((CELLS, 128), jnp.int32),
-            pltpu.SemaphoreType.DMA((8,)),
+            pltpu.SemaphoreType.DMA((9,)),
             pltpu.SemaphoreType.DMA((8,)),
             pltpu.SemaphoreType.DMA((8,)),
             pltpu.SemaphoreType.DMA((GROUPS,)),

time: 17.7 us -> 17.7 us (level)
  no operation moved by 1% of the time
where the time goes in v8:
time: 17.7 us; the launch traced here: 17.5 us
  Pallas kernels  16.2 us (92%)
  between operations  0.66 us (4%)
  local copies, waits for them, and re-layouts  0.61 us (3%)
    pallas_call x1, Pallas kernels, on_device(): pl.pallas_call(functools.partial(kernel, across), out_shape=jax.ShapeDtyp...  16.2 us
    unnamed x1, local copies, waits for them, and re-layouts  0.61 us

profile of v8, /device:TPU:35, one launch (start us, length us, event | category | flops | bytes accessed | tf_op | source)
XLA Modules:
  0.0 17.5 jit_solution(2327357366785327638)
XLA Ops:
  0.7 16.2 %shard_map.91 = bf16[2,32,128]{2,1,0:T(8,128)(2,1)S(1)} custom-call(s32[1,256]{1,0:T(1,128)} %bitcast.13, s32[1]{0:T(128)S(6)} %copy.11.count_ref, bf16[256,256]{1,0:T(8,128)(2,1)} %bitcast.10, bf16[256,128]{1,0:T(8,128)(2,1)} %bitcast.11, bf16[2304,128]{1,0:T(8,128)(2,1)} %bitcast.9, f32[128,40]{1,0:T(8,128)} %bitcast.12, ...), custom_call_target="tpu_custom_call" | custom-call | tf_op jit(solution)/shard_map/pallas_call | solution.py:545
  16.9 0.6 %copy.12 = bf16[2,128,32]{1,2,0:T(8,128)(2,1)} copy(bf16[2,128,32]{1,2,0:T(8,128)(2,1)S(1)} %bitcast.8) | data formatting | bytes 32768

commit v9 on v8

--- a/solution.py
+++ b/solution.py
@@ -234,30 +234,13 @@
     for copy in loads[1:6]:
         copy.start()
 
+    loads[0].wait()
+    loads[8].wait()
+    ops[group] = jnp.transpose(trans[...])
+
     @pl.when(earlier > 0)
     def _():
         pl.semaphore_wait(barrier, earlier)
-
-    for other in range(GROUPS):
-
-        @pl.when(other < group)
-        def _():
-            pl.semaphore_signal(
-                above_sem.at[group], inc=1, device_id=peer(other), device_id_type=MESH
-            )
-
-    for number in range(8):
-        there, before, device = beside(number)
-
-        @pl.when(there & before)
-        def _():
-            pl.semaphore_signal(
-                next_sem.at[number ^ 1], inc=1, device_id=device, device_id_type=MESH
-            )
-
-    loads[0].wait()
-    loads[8].wait()
-    ops[group] = jnp.transpose(trans[...])
 
     def send_ops(other):
         return pltpu.make_async_remote_copy(
@@ -274,6 +257,24 @@
         @pl.when(other < group)
         def _():
             send_ops(other).start()
+
+    for other in range(GROUPS):
+
+        @pl.when(other < group)
+        def _():
+            pl.semaphore_signal(
+                above_sem.at[group], inc=1, device_id=peer(other), device_id_type=MESH
+            )
+
+    for number in range(8):
+        there, before, device = beside(number)
+
+        @pl.when(there & before)
+        def _():
+            pl.semaphore_signal(
+                next_sem.at[number ^ 1], inc=1, device_id=device, device_id_type=MESH
+            )
+
 
     for copy in loads[6:8]:
         copy.start()

time: 17.7 us -> 17.7 us (level)
  no operation moved by 1% of the time
where the time goes in v9:
time: 17.7 us; the launch traced here: 17.5 us
  Pallas kernels  16.2 us (92%)
  between operations  0.66 us (4%)
  local copies, waits for them, and re-layouts  0.61 us (3%)
    pallas_call x1, Pallas kernels, on_device(): pl.pallas_call(functools.partial(kernel, across), out_shape=jax.ShapeDtyp...  16.2 us
    unnamed x1, local copies, waits for them, and re-layouts  0.61 us

profile of v9, /device:TPU:35, one launch (start us, length us, event | category | flops | bytes accessed | tf_op | source)
XLA Modules:
  0.0 17.5 jit_solution(12331394620876372282)
XLA Ops:
  0.7 16.2 %shard_map.91 = bf16[2,32,128]{2,1,0:T(8,128)(2,1)S(1)} custom-call(s32[1,256]{1,0:T(1,128)} %bitcast.13, s32[1]{0:T(128)S(6)} %copy.11.count_ref, bf16[256,256]{1,0:T(8,128)(2,1)} %bitcast.10, bf16[256,128]{1,0:T(8,128)(2,1)} %bitcast.11, bf16[2304,128]{1,0:T(8,128)(2,1)} %bitcast.9, f32[128,40]{1,0:T(8,128)} %bitcast.12, ...), custom_call_target="tpu_custom_call" | custom-call | tf_op jit(solution)/shard_map/pallas_call | solution.py:546
  16.9 0.6 %copy.12 = bf16[2,128,32]{1,2,0:T(8,128)(2,1)} copy(bf16[2,128,32]{1,2,0:T(8,128)(2,1)S(1)} %bitcast.8) | data formatting | bytes 32768

commit v10 on v9

--- a/solution.py
+++ b/solution.py
@@ -256,12 +256,6 @@
 
         @pl.when(other < group)
         def _():
-            send_ops(other).start()
-
-    for other in range(GROUPS):
-
-        @pl.when(other < group)
-        def _():
             pl.semaphore_signal(
                 above_sem.at[group], inc=1, device_id=peer(other), device_id_type=MESH
             )
@@ -275,6 +269,11 @@
                 next_sem.at[number ^ 1], inc=1, device_id=device, device_id_type=MESH
             )
 
+    for other in range(GROUPS):
+
+        @pl.when(other < group)
+        def _():
+            send_ops(other).start()
 
     for copy in loads[6:8]:
         copy.start()

time: 17.7 us -> 17.7 us (level)
  no operation moved by 1% of the time
where the time goes in v10:
time: 17.7 us; the launch traced here: 17.5 us
  Pallas kernels  16.2 us (92%)
  between operations  0.66 us (4%)
  local copies, waits for them, and re-layouts  0.61 us (3%)
    pallas_call x1, Pallas kernels, on_device(): pl.pallas_call(functools.partial(kernel, across), out_shape=jax.ShapeDtyp...  16.2 us
    unnamed x1, local copies, waits for them, and re-layouts  0.61 us

profile of v10, /device:TPU:35, one launch (start us, length us, event | category | flops | bytes accessed | tf_op | source)
XLA Modules:
  0.0 17.5 jit_solution(14129987640650158826)
XLA Ops:
  0.7 16.2 %shard_map.91 = bf16[2,32,128]{2,1,0:T(8,128)(2,1)S(1)} custom-call(s32[1,256]{1,0:T(1,128)} %bitcast.13, s32[1]{0:T(128)S(6)} %copy.11.count_ref, bf16[256,256]{1,0:T(8,128)(2,1)} %bitcast.10, bf16[256,128]{1,0:T(8,128)(2,1)} %bitcast.11, bf16[2304,128]{1,0:T(8,128)(2,1)} %bitcast.9, f32[128,40]{1,0:T(8,128)} %bitcast.12, ...), custom_call_target="tpu_custom_call" | custom-call | tf_op jit(solution)/shard_map/pallas_call | solution.py:545
  16.9 0.6 %copy.12 = bf16[2,128,32]{1,2,0:T(8,128)(2,1)} copy(bf16[2,128,32]{1,2,0:T(8,128)(2,1)S(1)} %bitcast.8) | data formatting | bytes 32768
